TPU v7x, 512 devices: a whole 4x4x16 slice. The times are simulated.
512 devices in a mesh: slab: 16 (over y, x), sta: 32 (over z, core).
Axes of the slice: x: 4, y: 4, z: 16, core: 2. Of those that a mesh axis runs over, the one named last changes fastest.
Arguments:
- station_place: float32 [128, 2], P('sta'), may hold values from 0 to 1
- station_height: float32 [128], P('sta'), may hold values from 2 to 8
- cell_weight: float32 [256, 256, 64], P('slab'), may hold values from 0.5 to 2
- kept: int32 [16, 128, 16], P('slab', 'sta'), may hold values from 0 to 2047, as said below
- dest: int32 [16, 128, 16, 1], P('slab', 'sta'), may hold values from 0 to 31; in each aligned block of 64 rows (0 to 63, 64 to 127, ..., all dimensions but the last counted through in order) at most 6 rows name the same one
Outputs:
- owned_blocks: float32 [16, 32, 32, 6, 128], P('slab', 'sta')
Inputs may be any that keep to these rules, and one draw needn't show every extreme that they name: `dest`: in the rows of one device (aligned blocks of 64 rows, in order), each owner is named by at most 6 rows, a bound that some block reaches. Let a = k // (256 / (2 * 16)) for a kept id k, and let x-slab p hold x from p * 256 / 16 on, 256 / 16 of them. When a >= 16, the cells on which row a of H(256) is nonzero lie in one x-slab. Among the 64 ids of one y-slab and one index of sta, at most 8 ids with a >= 16 touch any one x-slab, and some x-slab is touched by exactly 8.
All inputs are finite; a program needn't handle non-finite values.
Results may differ from a plain program's by a relative error of at most 0.0003.
Values sent between devices are 32-bit elements; how exact they have to be, the bound alone decides.
No kernel may reach another device: no remote copies, remote signals or barrier semaphores. Data moves between devices by JAX's collectives and lax.ppermute only.
A program may use at most 64 MiB of HBM per device.

v0:
```python
import jax
import jax.numpy as jnp
from jax import lax
from jax.sharding import PartitionSpec as P

kernel_scale = 32.0
root_half = 0.7071067811865476


def laid_out(tiles, dim):
    dims = list(tiles.shape[1:])
    dims[dim] *= tiles.shape[0]
    return jnp.moveaxis(tiles, 0, dim).reshape(dims)


def from_everyone(x, axis):
    peers = lax.axis_size(axis)
    return lax.all_to_all(jnp.broadcast_to(x[None], (peers, *x.shape)), axis, 0, 0, tiled=True)


def gathered_copies(x, axis, dim):
    return laid_out(from_everyone(x, axis), dim)


def in_blocks(x, dim, peers):
    dims = x.shape
    tiles = x.reshape(*dims[:dim], peers, dims[dim] // peers, *dims[dim + 1 :])
    return jnp.moveaxis(tiles, dim, 0)


def sent_and_summed(x, axis, dim):
    peers = lax.axis_size(axis)
    tiles = lax.all_to_all(in_blocks(x, dim, peers), axis, 0, 0, tiled=True)
    return jnp.sum(tiles, axis=0)


def haar(order):
    matrix = jnp.eye(order, dtype=jnp.float32)
    rows = jnp.arange(order, dtype=jnp.int32)[:, None]
    cols = jnp.arange(order, dtype=jnp.int32)[None, :]
    active = order
    while active % 2 == 0 and active > 1:
        half = active // 2
        low = (rows < half) & ((cols == 2 * rows) | (cols == 2 * rows + 1))
        upper = (rows >= half) & (rows < active)
        plus = upper & (cols == 2 * (rows - half))
        minus = upper & (cols == 2 * (rows - half) + 1)
        keeps = (rows >= active) & (rows == cols)
        step = (
            jnp.where(low | plus, root_half, 0.0)
            - jnp.where(minus, root_half, 0.0)
            + jnp.where(keeps, 1.0, 0.0)
        ).astype(jnp.float32)
        matrix = jnp.dot(
            step, matrix, precision=lax.Precision.HIGHEST, preferred_element_type=jnp.float32
        )
        active = half
    return matrix


def kernel(place, height, weight, xs, nx, ny, nz):
    ys = jnp.arange(ny, dtype=jnp.int32).astype(jnp.float32) + 0.5
    zs = jnp.arange(nz, dtype=jnp.int32).astype(jnp.float32) + 0.5
    east = xs[None, :] - place[:, 0:1] * nx
    north = ys[None, :] - place[:, 1:2] * ny
    depth = zs[None, :] + height[:, None]
    radius = (
        east[:, :, None, None] ** 2 + north[:, None, :, None] ** 2 + depth[:, None, None, :] ** 2
    )
    return kernel_scale * weight[None] * depth[:, None, None, :] / (radius * jnp.sqrt(radius))


def local(station_place, station_height, cell_weight, kept, dest):
    slab_count = lax.axis_size("slab")
    owner_count = lax.axis_size("sta")
    x_local, y_cells, z_cells = cell_weight.shape
    x_cells = x_local * slab_count
    stations = station_place.shape[0]
    keep = kept.shape[2]
    block = 2 * z_cells
    wx, wy, wz = (haar(x_cells), haar(y_cells), haar(z_cells))
    offset = lax.axis_index("slab") * x_local
    xs = (offset + jnp.arange(x_local, dtype=jnp.int32)).astype(jnp.float32) + 0.5
    field = kernel(station_place, station_height, cell_weight, xs, x_cells, y_cells, z_cells)
    field = jnp.einsum("sxyz,cz->sxyc", field, wz, precision=lax.Precision.HIGHEST)
    field = jnp.einsum("by,sxyc->sxbc", wy, field, precision=lax.Precision.HIGHEST)
    half = y_cells // slab_count // 2
    per_row = stations * keep
    all_ids = gathered_copies(kept, "slab", 0)
    all_ids = jnp.transpose(all_ids, (1, 0, 2))
    xrow = (all_ids // half).reshape(stations, -1)
    slab_ids = jnp.arange(slab_count, dtype=jnp.int32)[None, :, None]
    ypair = (slab_ids * half + all_ids % half).reshape(stations, -1)
    paired = field.reshape(stations, x_local, y_cells // 2, block)
    gathered = jax.vmap(lambda table, ids: table[:, ids, :])(paired, ypair)
    local_rows = lax.dynamic_slice_in_dim(wx, offset, x_local, 1)
    weights = local_rows[xrow]
    partial_value = jnp.einsum("smx,sxmc->smc", weights, gathered, precision=lax.Precision.HIGHEST)
    partial_value = partial_value.reshape(stations, slab_count, keep, block)
    picked = sent_and_summed(partial_value, "slab", 1)[:, 0]
    capacity = max(2, 3 * per_row // owner_count)
    owner = dest.reshape(per_row)
    values = picked.reshape(per_row, block)
    owners = jnp.arange(owner_count, dtype=jnp.int32)
    onehot = (owner[:, None] == owners[None, :]).astype(jnp.int32)
    slot = jnp.sum((jnp.cumsum(onehot, axis=0) - onehot) * onehot, axis=1)
    outgoing_rows = (
        jnp.zeros((owner_count, capacity, block), jnp.float32).at[owner, slot].set(values)
    )
    return lax.all_to_all(
        outgoing_rows[None, :, None], "sta", split_axis=1, concat_axis=2, tiled=True
    )


def solution(mesh):
    placed = (
        P("sta", None),
        P("sta"),
        P("slab", None, None),
        P("slab", "sta", None),
        P("slab", "sta", None, None),
    )
    return jax.shard_map(
        local,
        mesh=mesh,
        in_specs=placed,
        out_specs=P("slab", "sta", None, None, None),
        check_vma=False,
    )
```

profile of v0, /device:TPU:1, one launch (start us, length us, event | category | flops | bytes accessed | tf_op | source)
XLA Modules:
  0.0 134.0 jit_solution(2761427967140884088)
XLA Ops:
  0.0 1.3 broadcast_in_dim.188
  1.3 7.6 %all-to-all-start = ((s32[16,1,4,16]{3,2,1,0:T(4,128)}), s32[16,1,4,16]{3,2,1,0:T(4,128)S(1)}, u32[]{:S(2)}, u32[]{:S(2)}) async-start(s32[16,1,4,16]{3,2,1,0:T(4,128)} %broadcast_in_dim.188), calls=%async_computation | async-start | bytes 65536 | tf_op jit(solution)/shard_map/all_to_all | solution.py:18
  9.5 0.8 multiply_bitcast_fusion.1
  10.2 1.3 broadcast_multiply_fusion
  11.6 0.1 subtract_multiply_fusion.1
  11.6 0.1 subtract_multiply_fusion
  11.7 0.1 broadcast_add_fusion
  11.8 0.7 broadcast_add_fusion.1
  12.5 0.3 fusion.189
  12.8 0.3 fusion.195
  13.1 0.3 fusion.201
  13.3 0.3 fusion.207
  13.6 0.3 fusion.213
  13.9 0.3 convolution_bitcast_fusion.1
  14.2 5.9 %fusion.1 = f32[4,16,256,64]{2,3,1,0:T(8,128)S(1)} fusion(f32[64,64,1,1]{1,0,3,2:T(8,128)S(1)} %convolution_bitcast_fusion.1, f32[4,64]{1,0:T(4,128)S(1)} %get-tuple-element.8, f32[4,16,256]{2,1,0:T(8,128)S(1)} %broadcast_add_fusion, f32[4,64]{1,0:T(4,128)S(1)} %get-tuple-element.7, f32[16,256,64]{1,2,0:T(8,128)S(1)} %broadcast_multiply_fusion), kind=kOutput, calls=%fused_computation.5 | convolution fusion | flops 809500672 | bytes 5326848 | tf_op jit(solution)/shard_map/sxyz,cz->sxyc/dot_general | solution.py:85
  20.0 0.5 fusion.10
  20.5 0.9 fusion.16
  21.5 0.9 fusion.22
  22.4 0.9 fusion.28
  23.3 0.9 fusion.34
  24.3 0.9 fusion.40
  25.2 0.9 fusion.46
  26.2 0.9 fusion.52
  27.0 5.3 %convolution_bitcast_fusion = f32[4,16,256,64]{2,3,1,0:T(8,128)} fusion(f32[4,16,256,64]{2,3,1,0:T(8,128)S(1)} %fusion.1, f32[256,256]{0,1:T(8,128)S(1)} %fusion.52), kind=kOutput, calls=%fused_computation.8 | convolution fusion | flops 3221225472 | bytes 8650752 | tf_op jit(solution)/shard_map/by,sxyc->sxbc/dot_general | solution.py:86
  32.3 6.9 %copy.43 = f32[4,16,256,64]{3,2,1,0:T(8,128)} copy(f32[4,16,256,64]{2,3,1,0:T(8,128)} %convolution_bitcast_fusion) | data formatting | bytes 8388608 | tf_op jit(solution)/shard_map/by,sxyc->sxbc/transpose | solution.py:86
  39.2 7.2 %reshape.612 = f32[4,16,128,128]{3,2,1,0:T(8,128)} reshape(f32[4,16,256,64]{3,2,1,0:T(8,128)} %copy.43) | data formatting | bytes 8388608 | tf_op jit(solution)/shard_map/reshape | solution.py:94
  46.5 0.0 copy-start
  46.5 6.6 %copy.44 = f32[4,16,128,128]{3,1,2,0:T(8,128)} copy(f32[4,16,128,128]{3,2,1,0:T(8,128)} %reshape.612) | data formatting | bytes 8388608 | tf_op jit(solution)/shard_map/reshape | solution.py:94
  53.0 0.1 copy.41
  53.1 0.0 copy-done
  53.1 0.1 eq.329
  53.2 0.0 all-to-all-done
  53.2 0.1 fusion.187
  53.3 0.1 reshape.613
  53.4 0.1 reshape.611
  53.5 13.7 %gather_fusion.1 = f32[1024,16,128]{2,1,0:T(8,128)} fusion(f32[4,16,128,128]{3,1,2,0:T(8,128)} %copy.44, s32[1024]{0:T(1024)S(1)} %bitcast.93), kind=kCustom, calls=%fused_computation.1 | custom fusion | bytes 16785408 | tf_op jit(solution)/shard_map/vmap()/gather | solution.py:95
  67.2 2.8 %gather_fusion = f32[1024,16]{1,0:T(8,128)S(1)} fusion(f32[256,16]{1,0:T(8,128)S(1)} %copy.41, s32[1024]{0:T(1024)S(1)} %broadcast_clamp_fusion), kind=kCustom, calls=%fused_computation | custom fusion | bytes 135168 | tf_op jit(solution)/shard_map/gather | solution.py:97
  70.0 9.6 %fusion.398 = f32[4,256,1,128]{3,2,1,0:T(1,128)S(1)} fusion(f32[4,256,16,1]{2,3,1,0:T(1,128)S(1)} %bitcast.96, f32[4,16,256,128]{3,1,2,0:T(8,128)} %bitcast.94), kind=kOutput, calls=%fused_computation.474 | convolution fusion | flops 25165824 | bytes 8978432 | tf_op jit(solution)/shard_map/smx,sxmc->smc/dot_general | solution.py:98
  79.6 0.9 copy.45
  80.5 6.7 %all-to-all-start.1 = ((f32[16,4,1,16,128]{4,3,1,2,0:T(8,128)}), f32[16,4,1,16,128]{4,3,1,2,0:T(8,128)S(1)}, u32[]{:S(2)}, u32[]{:S(2)}) async-start(f32[16,4,1,16,128]{4,3,1,2,0:T(8,128)} %copy.45), calls=%async_computation.1 | async-start | bytes 1048576 | tf_op jit(solution)/shard_map/all_to_all | solution.py:33
  87.2 0.1 fusion.230
  87.2 0.1 reduce_window_sum.11
  87.3 0.5 broadcast.1101
  87.8 0.7 reduce.6
  88.5 0.1 reshape.609
  88.6 0.2 select_reduce_fusion
  88.8 7.4 %all-to-all-done.1 = f32[16,4,1,16,128]{4,3,1,2,0:T(8,128)S(1)} async-done(((f32[16,4,1,16,128]{4,3,1,2,0:T(8,128)}), f32[16,4,1,16,128]{4,3,1,2,0:T(8,128)S(1)}, u32[]{:S(2)}, u32[]{:S(2)}) %all-to-all-start.1) | async-done | bytes 524320 | tf_op jit(solution)/shard_map/all_to_all | solution.py:33
  96.2 3.7 %scatter_fusion = f32[32,6,128]{2,0,1:T(8,128)S(1)} fusion(f32[32,6,128]{2,0,1:T(8,128)S(1)} %broadcast_in_dim.183, s32[64]{0:T(128)S(1)} %fusion.330, f32[64,128]{1,0:T(8,128)S(1)} %bitcast.99), kind=kCustom, calls=%fused_computation.2 | custom fusion | bytes 98816 | tf_op jit(solution)/shard_map/scatter | solution.py:108
  100.0 0.1 copy.46
  100.1 33.3 %all_to_all.22 = f32[1,32,1,6,128]{4,2,3,0,1:T(1,128)S(1)} all-to-all(f32[1,32,1,6,128]{4,2,3,0,1:T(1,128)S(1)} %copy.46), channel_id=1, replica_groups=mesh['slab'=16,'sta'=32] {'sta'}, dimensions={1} | all-to-all | bytes 196608 | tf_op jit(solution)/shard_map/all_to_all | solution.py:110
  133.4 0.6 copy.47
  (57 shorter events, 0.4 us)
Async XLA Ops:
  1.3 51.9 %all-to-all-start = ((s32[16,1,4,16]{3,2,1,0:T(4,128)}), s32[16,1,4,16]{3,2,1,0:T(4,128)S(1)}, u32[]{:S(2)}, u32[]{:S(2)}) async-start(s32[16,1,4,16]{3,2,1,0:T(4,128)} %broadcast_in_dim.188), calls=%async_computation | async-start | bytes 65536 | tf_op jit(solution)/shard_map/all_to_all | solution.py:18
  46.5 6.7 %copy-start = (s32[1,4,16,1]{2,3,1,0:T(1,128)S(1)}, s32[1,4,16,1]{2,3,1,0:T(1,128)}, u32[]{:S(2)}) copy-start(s32[1,4,16,1]{2,3,1,0:T(1,128)} %param.9) | copy-start | bytes 772
  80.5 15.6 %all-to-all-start.1 = ((f32[16,4,1,16,128]{4,3,1,2,0:T(8,128)}), f32[16,4,1,16,128]{4,3,1,2,0:T(8,128)S(1)}, u32[]{:S(2)}, u32[]{:S(2)}) async-start(f32[16,4,1,16,128]{4,3,1,2,0:T(8,128)} %copy.45), calls=%async_computation.1 | async-start | bytes 1048576 | tf_op jit(solution)/shard_map/all_to_all | solution.py:33
where the time goes:
time: 135 us; the launch traced here: 134 us
  local copies, waits for them, and re-layouts  44.9 us (33%)
  blocking collectives  33.3 us (25%)
  matrix products  29.2 us (22%)
  starting transfers between devices  14.2 us (11%)
  waiting for transfers between devices  7.36 us (5%)
  other arithmetic  4.46 us (3%)
    all_to_all x1, blocking collectives, local(): lax.all_to_all(outgoing_rows[None, :, None], 'sta', split_axis=1, concat_...  33.3 us
    reshape x2, local copies, waits for them, and re-layouts, local(): paired = field.reshape(stations, x_local, y_cells // 2, block)  13.8 us
    gather x1, local copies, waits for them, and re-layouts, local(): gathered = jax.vmap(lambda table, ids: table[:, ids, :])(paired, ypair)  13.7 us
    dot_general x1, matrix products, local(): jnp.einsum('smx,sxmc->smc', weights, gathered, precision=lax.Precision.HI...  9.59 us
    dot_general x14, matrix products, haar(): jnp.dot(step, matrix, precision=lax.Precision.HIGHEST, preferred_element_...  8.53 us
    all_to_all x1, starting transfers between devices, from_everyone(): lax.all_to_all(jnp.broadcast_to(x[None], (peers, *x.shape)), axis, 0, 0,...  7.58 us
    all_to_all x1, waiting for transfers between devices, sent_and_summed(): tiles = lax.all_to_all(in_blocks(x, dim, peers), axis, 0, 0, tiled=True)  7.36 us
    transpose x1, local copies, waits for them, and re-layouts, local(): jnp.einsum('by,sxyc->sxbc', wy, field, precision=lax.Precision.HIGHEST)  6.92 us
  transfers between devices with their start and end apart: 2, of which 1 were waited for; matrix products, arithmetic and copies ran while one was open for 34% of the time, Pallas kernels for 0%

commit v1 on v0

v1 whole, which is shorter than its diff:
```python
import functools

import jax
import jax.numpy as jnp
import numpy as np
from jax import lax
from jax.experimental import pallas as pl
from jax.experimental.pallas import tpu as pltpu
from jax.sharding import PartitionSpec as P

SCALE = 32.0
SLABS = 16
OWNERS = 32
STA = 4
KEEP = 16
ROWS = STA * KEEP
XL = 16
NX = 256
NY = 256
NZ = 64
HALF = 8
CAP = 6
FINE = 8
COARSE = STA * HALF
MSG = COARSE + FINE
LANES = 2 * NZ
TABS = STA * XL
MIB = 1 << 20


def signs(order):
    out = np.zeros((order, order), np.float32)
    out[0] = 1
    count = 1
    while count < order:
        width = order // count
        for k in range(count):
            out[count + k, k * width : k * width + width // 2] = 1
            out[count + k, k * width + width // 2 : (k + 1) * width] = -1
        count *= 2
    return out


def constants():
    sy = signs(NY)
    sy = np.concatenate([sy[0::2], sy[1::2]], axis=0)
    sy = np.concatenate([sy, sy], axis=1)
    sz = np.zeros((LANES, LANES), np.float32)
    sz[:NZ, :NZ] = signs(NZ).T
    sz[NZ:, NZ:] = signs(NZ).T
    sz = np.concatenate([sz] * 3, axis=0)
    sx = np.repeat(signs(SLABS), COARSE, axis=1)
    bf = jnp.bfloat16
    return np.asarray(sy, bf), np.asarray(sz, bf), np.asarray(sx, bf)


def slab_pos():
    return lax.axis_index("slab")


def iota(shape, dim):
    return lax.broadcasted_iota(jnp.int32, shape, dim)


def column(tile):
    eye = iota((KEEP, KEEP), 0) == iota((KEEP, KEEP), 1)
    parts = []
    for s in range(STA):
        row = jnp.broadcast_to(tile[s : s + 1, :], (KEEP, KEEP))
        parts.append(jnp.sum(jnp.where(eye, row, 0.0), axis=1, keepdims=True))
    return jnp.concatenate(parts, axis=0)


def turned(col):
    eye = iota((ROWS, ROWS), 0) == iota((ROWS, ROWS), 1)
    wide = jnp.broadcast_to(col, (ROWS, ROWS))
    return jnp.sum(jnp.where(eye, wide, 0.0), axis=0, keepdims=True)


def earlier(col):
    row = turned(col)
    before = iota((ROWS, ROWS), 1) < iota((ROWS, ROWS), 0)
    same = (jnp.broadcast_to(row, (ROWS, ROWS)) == jnp.broadcast_to(col, (ROWS, ROWS))) & before
    return jnp.sum(jnp.where(same, 1.0, 0.0), axis=1, keepdims=True)


def split(x, parts):
    out = []
    for i in range(parts):
        piece = x.astype(jnp.bfloat16)
        out.append(piece)
        if i + 1 < parts:
            x = x - piece.astype(jnp.float32)
    return out


def places_of(k):
    a = lax.shift_right_logical(k, 3)
    pair = k & (HALF - 1)
    xs = jnp.full_like(a, SLABS)
    tab = jnp.full_like(a, XL - 1)
    for least, shift, base in ((16, 0, 14), (32, 1, 12), (64, 2, 8), (128, 3, 0)):
        inside = a >= least
        off = a - least
        xs = jnp.where(inside, lax.shift_right_logical(off, shift), xs)
        tab = jnp.where(inside, base + (off & ((1 << shift) - 1)), tab)
    return a, pair, xs, tab


def station_col():
    return lax.shift_right_logical(iota((ROWS, 1), 0), 4)


def list_kernel(kept_ref, out_ref):
    k = column(kept_ref[...].astype(jnp.float32)).astype(jnp.int32)
    _, pair, xs, tab = places_of(k)
    table = station_col() * XL + tab
    code = (table & 1) * 256 + lax.shift_right_logical(table, 1) * HALF + pair
    rank = earlier(xs.astype(jnp.float32)).astype(jnp.int32)
    key = turned((xs * FINE + rank).astype(jnp.float32)).astype(jnp.int32)
    coderow = turned(code.astype(jnp.float32))
    count = SLABS * FINE
    hit = jnp.broadcast_to(key, (count, ROWS)) == iota((count, ROWS), 0)
    found = jnp.sum(jnp.where(hit, jnp.broadcast_to(coderow, (count, ROWS)) + 1.0, 0.0), axis=1, keepdims=True)
    tile = jnp.broadcast_to(found - 1.0, (count, 128)).astype(jnp.int32)
    out_ref[...] = tile.reshape(SLABS, FINE, 128)


def table_kernel(place_ref, height_ref, w_ref, sy_ref, *refs):
    u_refs, g_ref = refs[:STA], refs[STA]
    first = (slab_pos() * XL).astype(jnp.float32)
    yy = iota((1, NY), 1).astype(jnp.float32) + 0.5
    rows = 16

    for s in range(STA):
        east0 = place_ref[0:1, s : s + 1] * float(NX)
        north2 = (yy - place_ref[1:2, s : s + 1] * float(NY)) ** 2
        height = height_ref[0:1, s : s + 1]

        def body(i, _):
            z0 = pl.multiple_of(i * rows, rows)
            zz = (z0 + iota((rows, 1), 0)).astype(jnp.float32) + 0.5 + height
            base = north2 + zz * zz
            lead = jnp.broadcast_to(SCALE * zz, (rows, NY))

            def leaf(x):
                east = (first + (x + 0.5)) - east0
                r = lax.rsqrt(base + east * east)
                return (w_ref[x, pl.ds(z0, rows), :] * lead) * (r * r * r)

            def put(tab, value):
                at = pl.ds(pl.multiple_of((s * XL + tab) * NZ + z0, rows), rows)
                high, low = split(value, 2)
                g_ref[at, 0:NY] = high
                g_ref[at, NY : 2 * NY] = low

            def tree(x, width):
                if width == 1:
                    return leaf(x)
                left = tree(x, width // 2)
                right = tree(x + width // 2, width // 2)
                start = {2: 0, 4: 8, 8: 12, 16: 14}[width]
                put(start + x // width, left - right)
                return left + right

            put(XL - 1, tree(0, XL))
            return 0

        lax.fori_loop(0, NZ // rows, body, 0)

    for i in range(TABS * NZ // 256):
        s, at = divmod(i * 256, XL * NZ)
        u_refs[s][:, at : at + 256] = lax.dot_general(
            sy_ref[...],
            g_ref[i * 256 : (i + 1) * 256, :],
            (((1,), (1,)), ((), ())),
            preferred_element_type=jnp.float32,
        )


def message_kernel(code_ref, *refs):
    u_refs, out_ref = refs[:STA], refs[STA]
    half_y = NY // 2
    low_half = iota((8, 128), 1) < NZ
    column_id = iota((FINE, 256), 1)

    def body(j, _):
        at = pl.multiple_of(j * HALF, HALF)
        at1 = pl.multiple_of(half_y + j * HALF, HALF)
        for s in range(STA):
            lanes = slice((XL - 2) * NZ, XL * NZ)
            u0 = u_refs[s][pl.ds(at, HALF), lanes]
            u1 = u_refs[s][pl.ds(at1, HALF), lanes]
            out_ref[j, s * HALF : (s + 1) * HALF, :] = jnp.where(low_half, pltpu.roll(u0, NZ, 1), u1)
        both = []
        for t in (at, at1):
            both.append(
                jnp.concatenate(
                    [u[pl.ds(t, HALF), q * 128 : (q + 1) * 128] for u in u_refs for q in range(XL // 2)], axis=0
                )
            )
        table = jnp.concatenate(both, axis=1)
        high, low = split(table, 2)
        code = code_ref[j]
        wide = jnp.concatenate([code, code], axis=1)
        known = jnp.where(wide >= 0, wide & 255, -1)
        pick = jnp.where(known == column_id, 1.0, 0.0).astype(jnp.bfloat16)
        got = jnp.dot(pick, high, preferred_element_type=jnp.float32)
        got = got + jnp.dot(pick, low, preferred_element_type=jnp.float32)
        v0, v1 = got[:, :128], got[:, 128:]
        even = jnp.where(low_half, v0, pltpu.roll(v1, NZ, 1))
        odd = jnp.where(low_half, pltpu.roll(v0, NZ, 1), v1)
        out_ref[j, COARSE:MSG, :] = jnp.where(code >= 256, odd, even)
        return 0

    lax.fori_loop(0, SLABS, body, 0, unroll=2)


def power(level_top, value):
    out = jnp.full(value.shape, 2.0 ** (-level_top / 2), jnp.float32)
    for level in range(1, level_top):
        out = jnp.where(value >= (1 << level), np.float32(2.0 ** (-(level_top - level) / 2)), out)
    return out


def index_kernel(kept_ref, dest_ref, sx_ref, coarse_ref, fine_ref, spot_ref, scale_ref):
    k = column(kept_ref[...].astype(jnp.float32)).astype(jnp.int32)
    a, pair, xs, _ = places_of(k)
    rank = earlier(xs.astype(jnp.float32)).astype(jnp.int32)
    one_a = jnp.where(iota((ROWS, SLABS), 1) == a, 1.0, 0.0).astype(jnp.bfloat16)
    sign = jnp.dot(one_a, sx_ref[...], preferred_element_type=jnp.float32)
    mine = station_col() * HALF + pair
    there = (iota((ROWS, SLABS * COARSE), 1) & (COARSE - 1)) == mine
    coarse_ref[...] = jnp.where(there, sign, 0.0).astype(jnp.bfloat16)
    key = jnp.where(xs < SLABS, xs * FINE + rank, -1)
    fine_ref[...] = jnp.where(iota((ROWS, SLABS * FINE), 1) == key, 1.0, 0.0).astype(jnp.bfloat16)
    dest = column(dest_ref[...].astype(jnp.float32))
    spot = turned(dest * 8.0 + earlier(dest)).astype(jnp.int32)
    where = jnp.broadcast_to(spot, (OWNERS * 8, ROWS)) == iota((OWNERS * 8, ROWS), 0)
    spot_ref[...] = jnp.where(where, 1.0, 0.0).astype(jnp.bfloat16)
    b = 2 * (slab_pos() * HALF + pair)
    rowscale = power(8, a) * power(8, b)
    lanescale = power(6, iota((ROWS, LANES), 1) & (NZ - 1))
    scale_ref[...] = rowscale * lanescale


def dots(pick, parts):
    total = jnp.dot(pick, parts[0], preferred_element_type=jnp.float32)
    for part in parts[1:]:
        total = total + jnp.dot(pick, part, preferred_element_type=jnp.float32)
    return total


def combine_kernel(got_ref, coarse_ref, fine_ref, spot_ref, scale_ref, sz_ref, out_ref):
    coarse = got_ref[:, 0:COARSE, :].reshape(SLABS * COARSE, LANES)
    fine = got_ref[:, COARSE:MSG, :].reshape(SLABS * FINE, LANES)
    value = dots(coarse_ref[...], split(coarse, 3)) + dots(fine_ref[...], split(fine, 3))
    value = jnp.dot(jnp.concatenate(split(value, 3), axis=1), sz_ref[...], preferred_element_type=jnp.float32)
    value = value * scale_ref[...]
    placed = dots(spot_ref[...], split(value, 3))
    out_ref[...] = placed.reshape(OWNERS, 8, LANES)


def call(body, outs, scratch=(), cost=None, limit=16):
    vmem = pl.BlockSpec(memory_space=pltpu.VMEM)
    many = isinstance(outs, (list, tuple))
    return functools.partial(
        pl.pallas_call,
        body,
        out_shape=outs,
        out_specs=[vmem] * len(outs) if many else vmem,
        scratch_shapes=list(scratch),
        compiler_params=pltpu.CompilerParams(vmem_limit_bytes=limit * MIB),
        cost_estimate=cost,
    )


def run(make, *args):
    vmem = pl.BlockSpec(memory_space=pltpu.VMEM)
    return make(in_specs=[vmem] * len(args))(*args)


def struct(shape, dtype=jnp.float32):
    return jax.ShapeDtypeStruct(shape, dtype)


def lists(kept):
    return run(call(list_kernel, struct((SLABS, FINE, 128), jnp.int32)), kept)


def tables(place, height, weight, sy):
    cost = pl.CostEstimate(flops=2 * 512 * 256 * 4096, bytes_accessed=6 * MIB, transcendentals=1 << 20)
    return run(
        call(
            table_kernel,
            [struct((NY, XL * NZ))] * STA,
            [pltpu.VMEM((TABS * NZ, 2 * NY), jnp.bfloat16)],
            cost,
        ),
        place.T,
        height.reshape(1, STA),
        jnp.transpose(weight, (0, 2, 1)),
        sy,
    )


def messages(codes, u):
    return run(call(message_kernel, struct((SLABS, MSG, LANES))), codes, *u)


def indices(kept, dest, sx):
    bf = jnp.bfloat16
    outs = [
        struct((ROWS, SLABS * COARSE), bf),
        struct((ROWS, SLABS * FINE), bf),
        struct((OWNERS * 8, ROWS), bf),
        struct((ROWS, LANES)),
    ]
    return run(call(index_kernel, outs), kept, dest, sx)


def combined(got, index, sz):
    return run(call(combine_kernel, struct((OWNERS, 8, LANES))), got, *index, sz)


def local(station_place, station_height, cell_weight, kept, dest):
    sy, sz, sx = (jnp.asarray(c) for c in constants())
    kept = kept.reshape(STA, KEEP)
    dest = dest.reshape(STA, KEEP)
    codes = lax.all_to_all(lists(kept), "slab", 0, 0, tiled=True)
    u = tables(station_place, station_height, cell_weight, sy)
    got = lax.all_to_all(messages(codes, u), "slab", 0, 0, tiled=True)
    index = indices(kept, dest, sx)
    out = lax.all_to_all(combined(got, index, sz), "sta", 0, 0, tiled=True)
    return out[None, None, :, :CAP, :]


def solution(mesh):
    placed = (
        P("sta", None),
        P("sta"),
        P("slab", None, None),
        P("slab", "sta", None),
        P("slab", "sta", None, None),
    )
    return jax.shard_map(
        local,
        mesh=mesh,
        in_specs=placed,
        out_specs=P("slab", "sta", None, None, None),
        check_vma=False,
    )
```

time: 135 us -> 72.1 us (0.53)
  local copies, waits for them, and re-layouts: 44.9 us -> 6.4 us
  matrix products: 29.2 us -> 0 us
  Pallas kernels: 0 us -> 9.8 us
  other arithmetic: 4.46 us -> 0 us
    dot_general x17 -> x0, matrix products: 29.2 us -> none  [the longest x1 9.59 us: local(): jnp.einsum('smx,sxmc->smc', weights, gathered, precision=lax.Precision.HI...]
    gather x2 -> x0, local copies, waits for them, and re-layouts: 16.5 us -> none  [the longest x1 13.7 us: local(): gathered = jax.vmap(lambda table, ids: table[:, ids, :])(paired, ypair)]
    reshape x5 -> x0, local copies, waits for them, and re-layouts: 14.1 us -> none  [the longest x2 13.8 us: local(): paired = field.reshape(stations, x_local, y_cells // 2, block)]
    pallas_call x0 -> x5, Pallas kernels: none -> 9.8 us  [run(): return make(in_specs=[vmem] * len(args))(*args)]
    transpose x2 -> x0, local copies, waits for them, and re-layouts: 7.79 us -> none  [the longest x1 6.92 us: local(): jnp.einsum('by,sxyc->sxbc', wy, field, precision=lax.Precision.HIGHEST)]
    unnamed x5 -> x22, local copies, waits for them, and re-layouts: 0.53 us -> 5.73 us
    scatter x1 -> x0, local copies, waits for them, and re-layouts: 3.75 us -> none  [local(): jnp.zeros((owner_count, capacity, block), jnp.float32).at[owner, slot]]
    mul x17 -> x0, other arithmetic: 2.17 us -> none  [the longest x1 1.32 us: kernel(): kernel_scale * weight[None] * depth[:, None, None, :]]
  transfers between devices with their start and end apart: 2 -> 2, of which waited for: 1 -> 1; matrix products, arithmetic and copies ran while one was open for 34% -> 0% of each run, Pallas kernels for 0% -> 7%
where the time goes in v1:
time: 72.1 us; the launch traced here: 71.7 us
  blocking collectives  33.5 us (46%)
  starting transfers between devices  14.4 us (20%)
  Pallas kernels  9.8 us (14%)
  waiting for transfers between devices  7.48 us (10%)
  local copies, waits for them, and re-layouts  6.4 us (9%)
    all_to_all x1, blocking collectives, local(): out = lax.all_to_all(combined(got, index, sz), 'sta', 0, 0, tiled=True)  33.5 us
    pallas_call x5, Pallas kernels, run(): return make(in_specs=[vmem] * len(args))(*args)  9.8 us
    all_to_all x1, starting transfers between devices, local(): codes = lax.all_to_all(lists(kept), 'slab', 0, 0, tiled=True)  7.58 us
    all_to_all x1, waiting for transfers between devices, local(): got = lax.all_to_all(messages(codes, u), 'slab', 0, 0, tiled=True)  7.48 us
    all_to_all x1, starting transfers between devices, local(): got = lax.all_to_all(messages(codes, u), 'slab', 0, 0, tiled=True)  6.8 us
    unnamed x22, local copies, waits for them, and re-layouts  5.73 us
  transfers between devices with their start and end apart: 2, of which 1 were waited for; matrix products, arithmetic and copies ran while one was open for 0% of the time, Pallas kernels for 7%

profile of v1, /device:TPU:1, one launch (start us, length us, event | category | flops | bytes accessed | tf_op | source)
XLA Modules:
  0.0 71.7 jit_solution(1090491304471626889)
XLA Ops:
  0.0 0.0 copy-start.4
  0.0 0.7 copy-done.4
  0.7 1.1 %shard_map.82 = s32[16,8,128]{2,1,0:T(8,128)} custom-call(s32[4,16]{1,0:T(4,128)S(1)} %bitcast.7), custom_call_target="tpu_custom_call" | custom-call | tf_op jit(solution)/shard_map/pallas_call | solution.py:280
  1.8 7.6 %all-to-all-start = ((s32[16,8,128]{2,1,0:T(8,128)}), s32[16,8,128]{2,1,0:T(8,128)S(1)}, u32[]{:S(2)}, u32[]{:S(2)}) async-start(s32[16,8,128]{2,1,0:T(8,128)} %shard_map.82), calls=%async_computation | async-start | bytes 131072 | tf_op jit(solution)/shard_map/all_to_all | solution.py:330
  9.4 0.0 copy-start.8
  9.4 0.0 copy-start.9
  9.4 0.7 copy-done.8
  10.1 0.0 copy-done.9
  10.1 0.0 copy-start.7
  10.1 1.2 %copy-done.7 = f32[16,256,64]{1,2,0:T(8,128)S(1)} copy-done((f32[16,256,64]{1,2,0:T(8,128)S(1)}, f32[16,256,64]{1,2,0:T(8,128)}, u32[]{:S(2)}) %copy-start.7) | copy-done | bytes 1048600
  11.3 0.0 copy-start.10
  11.3 0.9 %copy-done.10 = bf16[256,512]{1,0:T(8,128)(2,1)S(1)} copy-done((bf16[256,512]{1,0:T(8,128)(2,1)S(1)}, bf16[256,512]{1,0:T(8,128)(2,1)}, u32[]{:S(2)}) %copy-start.10) | copy-done | bytes 262168
  12.2 4.8 %shard_map.83 = (f32[256,1024]{1,0:T(8,128)S(1)}, f32[256,1024]{1,0:T(8,128)S(1)}, f32[256,1024]{1,0:T(8,128)S(1)}, f32[256,1024]{1,0:T(8,128)S(1)}) custom-call(f32[2,4]{1,0:T(2,128)S(1)} %bitcast.11, f32[1,4]{1,0:T(1,128)S(1)} %bitcast.12, f32[16,64,256]{2,1,0:T(8,128)S(1)} %bitcast.10, bf16[256,512]{1,0:T(8,128)(2,1)S(1)} %copy-done.10), custom_call_target="tpu_custom_call" | custom-call | flops 1073741824 | bytes 6291456 | tf_op jit(solution)/shard_map/pallas_call | solution.py:280
  17.0 0.0 copy-start
  17.0 1.0 %copy-done = f32[256,1024]{1,0:T(8,128)} copy-done((f32[256,1024]{1,0:T(8,128)}, f32[256,1024]{1,0:T(8,128)S(1)}, u32[]{:S(2)}) %copy-start) | copy-done | bytes 1048600
  18.0 0.0 all-to-all-done.code_ref
  18.0 0.0 copy-start.1
  18.0 1.2 %copy-done.1 = f32[256,1024]{1,0:T(8,128)S(1)} copy-done((f32[256,1024]{1,0:T(8,128)S(1)}, f32[256,1024]{1,0:T(8,128)}, u32[]{:S(2)}) %copy-start.1) | copy-done | bytes 1048600
  19.2 2.9 %shard_map.84 = f32[16,40,128]{2,1,0:T(8,128)} custom-call(s32[16,8,128]{2,1,0:T(8,128)S(1)} %all-to-all-done.code_ref, f32[256,1024]{1,0:T(8,128)S(1)} %get-tuple-element.13.refs_0_, f32[256,1024]{1,0:T(8,128)S(1)} %get-tuple-element.14.refs_1_, f32[256,1024]{1,0:T(8,128)S(1)} %get-tuple-element.15.refs_2_, f32[256,1024]{1,0:T(8,128)S(1)} %copy-done.1), custom_call_target="tpu_custom_call" | custom-call | tf_op jit(solution)/shard_map/pallas_call | solution.py:280
  22.1 0.0 copy-start.3
  22.1 0.0 copy-start.5
  22.1 0.0 copy-start.6
  22.1 0.0 copy-start.2
  22.2 6.8 %all-to-all-start.1 = ((f32[16,40,128]{2,1,0:T(8,128)}), f32[16,40,128]{2,1,0:T(8,128)S(1)}, u32[]{:S(2)}, u32[]{:S(2)}) async-start(f32[16,40,128]{2,1,0:T(8,128)} %shard_map.84), calls=%async_computation.1 | async-start | bytes 655360 | tf_op jit(solution)/shard_map/all_to_all | solution.py:332
  29.0 0.0 copy-done.3
  29.0 0.0 copy-done.5
  29.0 0.0 copy-done.6
  29.0 0.4 shard_map.85
  29.4 7.5 %all-to-all-done.1.got_ref = f32[16,40,128]{2,1,0:T(8,128)S(1)} async-done(((f32[16,40,128]{2,1,0:T(8,128)}), f32[16,40,128]{2,1,0:T(8,128)S(1)}, u32[]{:S(2)}, u32[]{:S(2)}) %all-to-all-start.1) | async-done | bytes 327712 | tf_op jit(solution)/shard_map/all_to_all | solution.py:332
  36.9 0.0 copy-done.2
  36.9 0.6 shard_map.86
  37.5 33.5 %all_to_all.15 = f32[32,8,128]{2,1,0:T(8,128)S(1)} all-to-all(f32[32,8,128]{2,1,0:T(8,128)S(1)} %shard_map.86), channel_id=1, replica_groups=mesh['slab'=16,'sta'=32] {'sta'}, dimensions={0} | all-to-all | bytes 262144 | tf_op jit(solution)/shard_map/all_to_all | solution.py:334
  71.0 0.7 copy.9
  (1 shorter events, 0.0 us)
Async XLA Ops:
  0.0 0.7 copy-start.4
  1.8 16.2 %all-to-all-start = ((s32[16,8,128]{2,1,0:T(8,128)}), s32[16,8,128]{2,1,0:T(8,128)S(1)}, u32[]{:S(2)}, u32[]{:S(2)}) async-start(s32[16,8,128]{2,1,0:T(8,128)} %shard_map.82), calls=%async_computation | async-start | bytes 131072 | tf_op jit(solution)/shard_map/all_to_all | solution.py:330
  9.4 0.7 copy-start.8
  9.4 0.7 copy-start.9
  10.1 1.2 %copy-start.7 = (f32[16,256,64]{1,2,0:T(8,128)S(1)}, f32[16,256,64]{1,2,0:T(8,128)}, u32[]{:S(2)}) copy-start(f32[16,256,64]{1,2,0:T(8,128)} %param.10) | copy-start | bytes 3145732
  11.3 0.9 %copy-start.10 = (bf16[256,512]{1,0:T(8,128)(2,1)S(1)}, bf16[256,512]{1,0:T(8,128)(2,1)}, u32[]{:S(2)}) copy-start(bf16[256,512]{1,0:T(8,128)(2,1)} %constant.6.clone.sy_ref) | copy-start | bytes 786436
  17.0 1.0 %copy-start = (f32[256,1024]{1,0:T(8,128)}, f32[256,1024]{1,0:T(8,128)S(1)}, u32[]{:S(2)}) copy-start(f32[256,1024]{1,0:T(8,128)S(1)} %get-tuple-element.16.refs_3_) | copy-start | bytes 3145732
  18.0 1.2 %copy-start.1 = (f32[256,1024]{1,0:T(8,128)S(1)}, f32[256,1024]{1,0:T(8,128)}, u32[]{:S(2)}) copy-start(f32[256,1024]{1,0:T(8,128)} %copy-done) | copy-start | bytes 3145732
  22.1 6.8 %copy-start.3 = (bf16[16,512]{1,0:T(8,128)(2,1)S(1)}, bf16[16,512]{1,0:T(8,128)(2,1)}, u32[]{:S(2)}) copy-start(bf16[16,512]{1,0:T(8,128)(2,1)} %constant.8.clone.sx_ref) | copy-start | bytes 49156
  22.1 6.8 %copy-start.5 = (s32[1,4,16]{2,1,0:T(4,128)S(1)}, s32[1,4,16]{2,1,0:T(4,128)}, u32[]{:S(2)}) copy-start(s32[1,4,16]{2,1,0:T(4,128)} %param.11) | copy-start | bytes 772
  22.1 6.8 %copy-start.6 = (s32[1,4,16,1]{2,3,1,0:T(1,128)S(1)}, s32[1,4,16,1]{2,3,1,0:T(1,128)}, u32[]{:S(2)}) copy-start(s32[1,4,16,1]{2,3,1,0:T(1,128)} %param.12) | copy-start | bytes 772
  22.1 14.7 %copy-start.2 = (bf16[384,128]{1,0:T(8,128)(2,1)S(1)}, bf16[384,128]{1,0:T(8,128)(2,1)}, u32[]{:S(2)}) copy-start(bf16[384,128]{1,0:T(8,128)(2,1)} %constant.7.clone.sz_ref) | copy-start | bytes 294916
  22.2 14.7 %all-to-all-start.1 = ((f32[16,40,128]{2,1,0:T(8,128)}), f32[16,40,128]{2,1,0:T(8,128)S(1)}, u32[]{:S(2)}, u32[]{:S(2)}) async-start(f32[16,40,128]{2,1,0:T(8,128)} %shard_map.84), calls=%async_computation.1 | async-start | bytes 655360 | tf_op jit(solution)/shard_map/all_to_all | solution.py:332

commit v2 on v1

--- a/solution.py
+++ b/solution.py
@@ -1,5 +1,3 @@
-import functools
-
 import jax
 import jax.numpy as jnp
 import numpy as np
@@ -26,6 +24,8 @@
 LANES = 2 * NZ
 TABS = STA * XL
 MIB = 1 << 20
+GRANT = 52000 << 10
+FAR = 30
 
 
 def signs(order):
@@ -44,7 +44,6 @@
 def constants():
     sy = signs(NY)
     sy = np.concatenate([sy[0::2], sy[1::2]], axis=0)
-    sy = np.concatenate([sy, sy], axis=1)
     sz = np.zeros((LANES, LANES), np.float32)
     sz[:NZ, :NZ] = signs(NZ).T
     sz[NZ:, NZ:] = signs(NZ).T
@@ -111,11 +110,15 @@
     return lax.shift_right_logical(iota((ROWS, 1), 0), 4)
 
 
-def list_kernel(kept_ref, out_ref):
+def list_kernel(kept_ref, place_ref, height_ref, sy_ref, out_ref, place_out, height_out, sy_out):
+    sy_out[...] = sy_ref[...]
+    place_out[...] = place_ref[...]
+    height_out[...] = height_ref[...]
     k = column(kept_ref[...].astype(jnp.float32)).astype(jnp.int32)
     _, pair, xs, tab = places_of(k)
     table = station_col() * XL + tab
-    code = (table & 1) * 256 + lax.shift_right_logical(table, 1) * HALF + pair
+    row = (slab_pos() & 1) * HALF + pair
+    code = (table & 1) * (16 * TABS // 2) + lax.shift_right_logical(table, 1) * 16 + row
     rank = earlier(xs.astype(jnp.float32)).astype(jnp.int32)
     key = turned((xs * FINE + rank).astype(jnp.float32)).astype(jnp.int32)
     coderow = turned(code.astype(jnp.float32))
@@ -126,19 +129,28 @@
     out_ref[...] = tile.reshape(SLABS, FINE, 128)
 
 
-def table_kernel(place_ref, height_ref, w_ref, sy_ref, *refs):
-    u_refs, g_ref = refs[:STA], refs[STA]
+PART = XL * NZ
+
+
+def table_kernel(place_ref, height_ref, w_hbm, sy_ref, far_ref, *refs):
+    outs = refs[: STA - 1]
+    w_ref, g_ref, own_ref, w_sems, sem = refs[STA - 1 :]
     first = (slab_pos() * XL).astype(jnp.float32)
     yy = iota((1, NY), 1).astype(jnp.float32) + 0.5
     rows = 16
-
-    for s in range(STA):
+    arrivals = []
+    for i in range(NZ // rows):
+        at = (slice(None), pl.ds(i * rows, rows))
+        arrivals.append(pltpu.make_async_copy(w_hbm.at[at], w_ref.at[at], w_sems.at[i]))
+        arrivals[-1].start()
+
+    def field(s):
         east0 = place_ref[0:1, s : s + 1] * float(NX)
         north2 = (yy - place_ref[1:2, s : s + 1] * float(NY)) ** 2
         height = height_ref[0:1, s : s + 1]
-
-        def body(i, _):
-            z0 = pl.multiple_of(i * rows, rows)
+        for z0 in range(0, NZ, rows):
+            if s == 0:
+                arrivals[z0 // rows].wait()
             zz = (z0 + iota((rows, 1), 0)).astype(jnp.float32) + 0.5 + height
             base = north2 + zz * zz
             lead = jnp.broadcast_to(SCALE * zz, (rows, NY))
@@ -146,10 +158,10 @@
             def leaf(x):
                 east = (first + (x + 0.5)) - east0
                 r = lax.rsqrt(base + east * east)
-                return (w_ref[x, pl.ds(z0, rows), :] * lead) * (r * r * r)
+                return (w_ref[x, z0 : z0 + rows, :] * lead) * (r * r * r)
 
             def put(tab, value):
-                at = pl.ds(pl.multiple_of((s * XL + tab) * NZ + z0, rows), rows)
+                at = slice((s * XL + tab) * NZ + z0, (s * XL + tab) * NZ + z0 + rows)
                 high, low = split(value, 2)
                 g_ref[at, 0:NY] = high
                 g_ref[at, NY : 2 * NY] = low
@@ -164,56 +176,86 @@
                 return left + right
 
             put(XL - 1, tree(0, XL))
-            return 0
-
-        lax.fori_loop(0, NZ // rows, body, 0)
-
-    for i in range(TABS * NZ // 256):
-        s, at = divmod(i * 256, XL * NZ)
-        u_refs[s][:, at : at + 256] = lax.dot_general(
-            sy_ref[...],
-            g_ref[i * 256 : (i + 1) * 256, :],
-            (((1,), (1,)), ((), ())),
-            preferred_element_type=jnp.float32,
-        )
-
-
-def message_kernel(code_ref, *refs):
-    u_refs, out_ref = refs[:STA], refs[STA]
-    half_y = NY // 2
-    low_half = iota((8, 128), 1) < NZ
-    column_id = iota((FINE, 256), 1)
-
-    def body(j, _):
-        at = pl.multiple_of(j * HALF, HALF)
-        at1 = pl.multiple_of(half_y + j * HALF, HALF)
-        for s in range(STA):
-            lanes = slice((XL - 2) * NZ, XL * NZ)
-            u0 = u_refs[s][pl.ds(at, HALF), lanes]
-            u1 = u_refs[s][pl.ds(at1, HALF), lanes]
-            out_ref[j, s * HALF : (s + 1) * HALF, :] = jnp.where(low_half, pltpu.roll(u0, NZ, 1), u1)
-        both = []
-        for t in (at, at1):
-            both.append(
-                jnp.concatenate(
-                    [u[pl.ds(t, HALF), q * 128 : (q + 1) * 128] for u in u_refs for q in range(XL // 2)], axis=0
+
+    def product(s):
+        to = outs[s - 1] if s else own_ref
+        for i in range(PART // 256):
+            g = g_ref[s * PART + i * 256 : s * PART + (i + 1) * 256, :]
+            u = lax.dot_general(
+                jnp.concatenate([sy_ref[...]] * 2, axis=1),
+                g,
+                (((1,), (1,)), ((), ())),
+                preferred_element_type=jnp.float32,
+            )
+            high, low = split(u, 2)
+            to[:, i * 256 : (i + 1) * 256] = high
+            to[:, PART + i * 256 : PART + (i + 1) * 256] = low
+
+    copy = pltpu.make_async_copy(own_ref, far_ref.at[0], sem)
+    for s in range(STA):
+        field(s)
+        if s:
+            product(s - 1)
+        if s == 1:
+            copy.start()
+    product(STA - 1)
+    copy.wait()
+
+
+def message_kernel(code_ref, far_ref, *refs):
+    u_refs, out_ref, near_ref, sem = refs[: STA - 1], refs[STA - 1], refs[STA], refs[STA + 1]
+    copy = pltpu.make_async_copy(far_ref.at[0], near_ref, sem)
+    copy.start()
+    low_half = iota((16, 128), 1) < NZ
+    column_id = iota((16, 256), 1)
+    groups = SLABS // 2
+
+    def rows_of(g, t):
+        return slice(t * (NY // 2) + g * 16, t * (NY // 2) + g * 16 + 16)
+
+    def known(g):
+        code = code_ref[2 * g : 2 * g + 2].reshape(16, 128)
+        wide = jnp.concatenate([code, code], axis=1)
+        return code, jnp.where(wide >= 0, wide & 511, -1)
+
+    def picked(g, tables, base):
+        pick = jnp.where(known(g)[1] == column_id + base, 1.0, 0.0).astype(jnp.bfloat16)
+        total = None
+        for part in (0, PART):
+            both = []
+            for t in (0, 1):
+                both.append(
+                    jnp.concatenate(
+                        [u[rows_of(g, t), part + q * 128 : part + (q + 1) * 128] for u in tables for q in range(XL // 2)],
+                        axis=0,
+                    )
                 )
-            )
-        table = jnp.concatenate(both, axis=1)
-        high, low = split(table, 2)
-        code = code_ref[j]
-        wide = jnp.concatenate([code, code], axis=1)
-        known = jnp.where(wide >= 0, wide & 255, -1)
-        pick = jnp.where(known == column_id, 1.0, 0.0).astype(jnp.bfloat16)
-        got = jnp.dot(pick, high, preferred_element_type=jnp.float32)
-        got = got + jnp.dot(pick, low, preferred_element_type=jnp.float32)
-        v0, v1 = got[:, :128], got[:, 128:]
+            got = jnp.dot(pick, jnp.concatenate(both, axis=1), preferred_element_type=jnp.float32)
+            total = got if total is None else total + got
+        return total
+
+    def coarse(g, s, u):
+        lanes = PART - 128
+        v = []
+        for t in (0, 1):
+            high = u[rows_of(g, t), lanes : lanes + 128].astype(jnp.float32)
+            v.append(high + u[rows_of(g, t), PART + lanes : PART + lanes + 128].astype(jnp.float32))
+        row = jnp.where(low_half, pltpu.roll(v[0], NZ, 1), v[1])
+        out_ref[2 * g : 2 * g + 2, s * HALF : (s + 1) * HALF, :] = row.reshape(2, HALF, 128)
+
+    got = [picked(g, u_refs[1:], 256) for g in range(groups)]
+    for g in range(groups):
+        for s in range(1, STA):
+            coarse(g, s, u_refs[s - 1])
+    copy.wait()
+    for g in range(groups):
+        coarse(g, 0, near_ref)
+        both = got[g] + picked(g, (near_ref, u_refs[0]), 0)
+        v0, v1 = both[:, :128], both[:, 128:]
         even = jnp.where(low_half, v0, pltpu.roll(v1, NZ, 1))
         odd = jnp.where(low_half, pltpu.roll(v0, NZ, 1), v1)
-        out_ref[j, COARSE:MSG, :] = jnp.where(code >= 256, odd, even)
-        return 0
-
-    lax.fori_loop(0, SLABS, body, 0, unroll=2)
+        fine = jnp.where(known(g)[0] >= 512, odd, even)
+        out_ref[2 * g : 2 * g + 2, COARSE:MSG, :] = fine.reshape(2, FINE, 128)
 
 
 def power(level_top, value):
@@ -261,51 +303,73 @@
     out_ref[...] = placed.reshape(OWNERS, 8, LANES)
 
 
-def call(body, outs, scratch=(), cost=None, limit=16):
-    vmem = pl.BlockSpec(memory_space=pltpu.VMEM)
-    many = isinstance(outs, (list, tuple))
-    return functools.partial(
-        pl.pallas_call,
+VMEM = pl.BlockSpec(memory_space=pltpu.VMEM)
+HBM = pl.BlockSpec(memory_space=pltpu.HBM)
+
+
+def run(body, args, ins, shapes, outs, scratch=(), cost=None, limit=16 * MIB):
+    return pl.pallas_call(
         body,
-        out_shape=outs,
-        out_specs=[vmem] * len(outs) if many else vmem,
+        out_shape=shapes,
+        in_specs=ins,
+        out_specs=outs,
         scratch_shapes=list(scratch),
-        compiler_params=pltpu.CompilerParams(vmem_limit_bytes=limit * MIB),
+        compiler_params=pltpu.CompilerParams(vmem_limit_bytes=limit),
         cost_estimate=cost,
-    )
-
-
-def run(make, *args):
-    vmem = pl.BlockSpec(memory_space=pltpu.VMEM)
-    return make(in_specs=[vmem] * len(args))(*args)
+    )(*args)
 
 
 def struct(shape, dtype=jnp.float32):
     return jax.ShapeDtypeStruct(shape, dtype)
 
 
-def lists(kept):
-    return run(call(list_kernel, struct((SLABS, FINE, 128), jnp.int32)), kept)
+def lists(kept, place, height, sy):
+    return run(
+        list_kernel,
+        (kept, place.T, height.reshape(1, STA), sy),
+        [VMEM] * 4,
+        [
+            struct((SLABS, FINE, 128), jnp.int32),
+            struct((2, STA)),
+            struct((1, STA)),
+            struct((NY, NY), jnp.bfloat16),
+        ],
+        [VMEM] * 4,
+    )
 
 
 def tables(place, height, weight, sy):
     cost = pl.CostEstimate(flops=2 * 512 * 256 * 4096, bytes_accessed=6 * MIB, transcendentals=1 << 20)
+    part = struct((NY, 2 * PART), jnp.bfloat16)
     return run(
-        call(
-            table_kernel,
-            [struct((NY, XL * NZ))] * STA,
-            [pltpu.VMEM((TABS * NZ, 2 * NY), jnp.bfloat16)],
-            cost,
-        ),
-        place.T,
-        height.reshape(1, STA),
-        jnp.transpose(weight, (0, 2, 1)),
-        sy,
+        table_kernel,
+        (place, height, jnp.transpose(weight, (0, 2, 1)), sy),
+        [VMEM, VMEM, HBM, VMEM],
+        [struct((FAR, NY, 2 * PART), jnp.bfloat16)] + [part] * (STA - 1),
+        [HBM] + [VMEM] * (STA - 1),
+        [
+            pltpu.VMEM((XL, NZ, NY), jnp.float32),
+            pltpu.VMEM((TABS * NZ, 2 * NY), jnp.bfloat16),
+            pltpu.VMEM((NY, 2 * PART), jnp.bfloat16),
+            pltpu.SemaphoreType.DMA((NZ // 16,)),
+            pltpu.SemaphoreType.DMA,
+        ],
+        cost,
+        GRANT,
     )
 
 
 def messages(codes, u):
-    return run(call(message_kernel, struct((SLABS, MSG, LANES))), codes, *u)
+    return run(
+        message_kernel,
+        (codes, *u),
+        [VMEM, HBM] + [VMEM] * (STA - 1),
+        struct((SLABS, MSG, LANES)),
+        VMEM,
+        [pltpu.VMEM((NY, 2 * PART), jnp.bfloat16), pltpu.SemaphoreType.DMA],
+        None,
+        44 * MIB,
+    )
 
 
 def indices(kept, dest, sx):
@@ -316,19 +380,20 @@
         struct((OWNERS * 8, ROWS), bf),
         struct((ROWS, LANES)),
     ]
-    return run(call(index_kernel, outs), kept, dest, sx)
+    return run(index_kernel, (kept, dest, sx), [VMEM] * 3, outs, [VMEM] * 4)
 
 
 def combined(got, index, sz):
-    return run(call(combine_kernel, struct((OWNERS, 8, LANES))), got, *index, sz)
+    return run(combine_kernel, (got, *index, sz), [VMEM] * 6, struct((OWNERS, 8, LANES)), VMEM)
 
 
 def local(station_place, station_height, cell_weight, kept, dest):
     sy, sz, sx = (jnp.asarray(c) for c in constants())
     kept = kept.reshape(STA, KEEP)
     dest = dest.reshape(STA, KEEP)
-    codes = lax.all_to_all(lists(kept), "slab", 0, 0, tiled=True)
-    u = tables(station_place, station_height, cell_weight, sy)
+    codes, place, height, sy = lists(kept, station_place, station_height, sy)
+    codes = lax.all_to_all(codes, "slab", 0, 0, tiled=True)
+    u = tables(place, height, cell_weight, sy)
     got = lax.all_to_all(messages(codes, u), "slab", 0, 0, tiled=True)
     index = indices(kept, dest, sx)
     out = lax.all_to_all(combined(got, index, sz), "sta", 0, 0, tiled=True)

time: 72.1 us -> 68.3 us (0.947)
  local copies, waits for them, and re-layouts: 6.4 us -> 3.63 us
  starting transfers between devices: 14.4 us -> 11.9 us
  waiting for transfers between devices: 7.48 us -> 9.83 us
  Pallas kernels: 9.8 us -> 8.93 us
    unnamed x22 -> x16, local copies, waits for them, and re-layouts: 5.73 us -> 2.96 us
    all_to_all x1, starting transfers between devices: 6.8 us -> 4.33 us  [local(): got = lax.all_to_all(messages(codes, u), 'slab', 0, 0, tiled=True)]
    all_to_all x1, waiting for transfers between devices: 0.01 us -> 2.35 us  [local(): codes = lax.all_to_all(codes, 'slab', 0, 0, tiled=True)]
    pallas_call x5, Pallas kernels: 9.8 us -> 8.93 us  [run(): pl.pallas_call(body, out_shape=shapes, in_specs=ins, out_specs=outs, scra...]
  transfers between devices with their start and end apart: 2 -> 2, of which waited for: 1 -> 2; matrix products, arithmetic and copies ran while one was open for 0% -> 0% of each run, Pallas kernels for 7% -> 7%
where the time goes in v2:
time: 68.3 us; the launch traced here: 67.9 us
  blocking collectives  33.5 us (49%)
  starting transfers between devices  11.9 us (17%)
  waiting for transfers between devices  9.83 us (14%)
  Pallas kernels  8.93 us (13%)
  local copies, waits for them, and re-layouts  3.63 us (5%)
    all_to_all x1, blocking collectives, local(): out = lax.all_to_all(combined(got, index, sz), 'sta', 0, 0, tiled=True)  33.5 us
    pallas_call x5, Pallas kernels, run(): pl.pallas_call(body, out_shape=shapes, in_specs=ins, out_specs=outs, scra...  8.93 us
    all_to_all x1, starting transfers between devices, local(): codes = lax.all_to_all(codes, 'slab', 0, 0, tiled=True)  7.58 us
    all_to_all x1, waiting for transfers between devices, local(): got = lax.all_to_all(messages(codes, u), 'slab', 0, 0, tiled=True)  7.48 us
    all_to_all x1, starting transfers between devices, local(): got = lax.all_to_all(messages(codes, u), 'slab', 0, 0, tiled=True)  4.33 us
    unnamed x16, local copies, waits for them, and re-layouts  2.96 us
    all_to_all x1, waiting for transfers between devices, local(): codes = lax.all_to_all(codes, 'slab', 0, 0, tiled=True)  2.35 us
  transfers between devices with their start and end apart: 2, of which 2 were waited for; matrix products, arithmetic and copies ran while one was open for 0% of the time, Pallas kernels for 7%

profile of v2, /device:TPU:1, one launch (start us, length us, event | category | flops | bytes accessed | tf_op | source)
XLA Modules:
  0.0 67.9 jit_solution(10674422152931220834)
XLA Ops:
  0.0 0.0 copy-start.4
  0.0 0.0 copy-start.5
  0.0 0.0 copy-start
  0.0 0.9 %copy-done = bf16[256,256]{1,0:T(8,128)(2,1)S(1)} copy-done((bf16[256,256]{1,0:T(8,128)(2,1)S(1)}, bf16[256,256]{1,0:T(8,128)(2,1)}, u32[]{:S(2)}) %copy-start) | copy-done | bytes 131096
  0.9 0.0 copy-start.3
  0.9 0.7 %copy-done.3 = s32[1,4,16]{2,1,0:T(4,128)S(1)} copy-done((s32[1,4,16]{2,1,0:T(4,128)S(1)}, s32[1,4,16]{2,1,0:T(4,128)}, u32[]{:S(2)}) %copy-start.3) | copy-done | bytes 280
  1.6 0.0 copy-start.6
  1.6 0.7 copy-done.6
  2.3 0.0 copy-start.7
  2.3 0.7 copy-done.7
  3.0 0.0 copy-start.2
  3.0 0.0 copy-start.1
  3.0 1.1 %shard_map.82 = (s32[16,8,128]{2,1,0:T(8,128)}, f32[2,4]{1,0:T(2,128)S(1)}, f32[1,4]{1,0:T(1,128)S(1)}, bf16[256,256]{1,0:T(8,128)(2,1)S(1)}) custom-call(s32[4,16]{1,0:T(4,128)S(1)} %bitcast.7, f32[2,4]{1,0:T(2,128)S(1)} %bitcast.10, f32[1,4]{1,0:T(1,128)S(1)} %bitcast.11, bf16[256,256]{1,0:T(8,128)(2,1)S(1)} %copy-done), custom_call_target="tpu_custom_call" | custom-call | tf_op jit(solution)/shard_map/pallas_call | solution.py:311
  4.1 7.6 %all-to-all-start = ((s32[16,8,128]{2,1,0:T(8,128)}), s32[16,8,128]{2,1,0:T(8,128)S(1)}, u32[]{:S(2)}, u32[]{:S(2)}) async-start(s32[16,8,128]{2,1,0:T(8,128)} %get-tuple-element.17), calls=%async_computation | async-start | bytes 131072 | tf_op jit(solution)/shard_map/all_to_all | solution.py:395
  11.7 4.2 %shard_map.83 = (bf16[30,256,2048]{2,1,0:T(8,128)(2,1)}, bf16[256,2048]{1,0:T(8,128)(2,1)S(1)}, bf16[256,2048]{1,0:T(8,128)(2,1)S(1)}, bf16[256,2048]{1,0:T(8,128)(2,1)S(1)}) custom-call(f32[2,4]{1,0:T(2,128)S(1)} %get-tuple-element.18.place_ref, f32[1,4]{1,0:T(1,128)S(1)} %get-tuple-element.19.height_ref, f32[16,64,256]{2,1,0:T(8,128)} %bitcast.12, ...), custom_call_target="tpu_custom_call" | custom-call | flops 1073741824 | bytes 6291456 | tf_op jit(solution)/shard_map/pallas_call | solution.py:311
  15.8 2.3 %all-to-all-done.code_ref = s32[16,8,128]{2,1,0:T(8,128)S(1)} async-done(((s32[16,8,128]{2,1,0:T(8,128)}), s32[16,8,128]{2,1,0:T(8,128)S(1)}, u32[]{:S(2)}, u32[]{:S(2)}) %all-to-all-start) | async-done | bytes 65568 | tf_op jit(solution)/shard_map/all_to_all | solution.py:395
  18.2 2.7 %shard_map.84 = f32[16,40,128]{2,1,0:T(8,128)} custom-call(s32[16,8,128]{2,1,0:T(8,128)S(1)} %all-to-all-done.code_ref, bf16[30,256,2048]{2,1,0:T(8,128)(2,1)} %get-tuple-element.21.far_ref, bf16[256,2048]{1,0:T(8,128)(2,1)S(1)} %get-tuple-element.22.refs_0_, bf16[256,2048]{1,0:T(8,128)(2,1)S(1)} %get-tuple-element.23.refs_1_, ...), custom_call_target="tpu_custom_call" | custom-call | tf_op jit(solution)/shard_map/pallas_call | solution.py:311
  20.8 4.3 %all-to-all-start.1 = ((f32[16,40,128]{2,1,0:T(8,128)}), f32[16,40,128]{2,1,0:T(8,128)S(1)}, u32[]{:S(2)}, u32[]{:S(2)}) async-start(f32[16,40,128]{2,1,0:T(8,128)} %shard_map.84), calls=%async_computation.1 | async-start | bytes 655360 | tf_op jit(solution)/shard_map/all_to_all | solution.py:397
  25.2 0.0 copy-done.4
  25.2 0.0 copy-done.5
  25.2 0.0 copy-done.2
  25.2 0.4 shard_map.85
  25.6 7.5 %all-to-all-done.1.got_ref = f32[16,40,128]{2,1,0:T(8,128)S(1)} async-done(((f32[16,40,128]{2,1,0:T(8,128)}), f32[16,40,128]{2,1,0:T(8,128)S(1)}, u32[]{:S(2)}, u32[]{:S(2)}) %all-to-all-start.1) | async-done | bytes 327712 | tf_op jit(solution)/shard_map/all_to_all | solution.py:397
  33.1 0.0 copy-done.1
  33.1 0.6 shard_map.86
  33.7 33.5 %all_to_all.15 = f32[32,8,128]{2,1,0:T(8,128)S(1)} all-to-all(f32[32,8,128]{2,1,0:T(8,128)S(1)} %shard_map.86), channel_id=1, replica_groups=mesh['slab'=16,'sta'=32] {'sta'}, dimensions={0} | all-to-all | bytes 262144 | tf_op jit(solution)/shard_map/all_to_all | solution.py:399
  67.2 0.7 copy.9
  (1 shorter events, 0.0 us)
Async XLA Ops:
  0.0 25.2 %copy-start.4 = (s32[1,4,16]{2,1,0:T(4,128)S(1)}, s32[1,4,16]{2,1,0:T(4,128)}, u32[]{:S(2)}) copy-start(s32[1,4,16]{2,1,0:T(4,128)} %param.11) | copy-start | bytes 772
  0.0 25.2 %copy-start.5 = (s32[1,4,16,1]{2,3,1,0:T(1,128)S(1)}, s32[1,4,16,1]{2,3,1,0:T(1,128)}, u32[]{:S(2)}) copy-start(s32[1,4,16,1]{2,3,1,0:T(1,128)} %param.12) | copy-start | bytes 772
  0.0 0.9 %copy-start = (bf16[256,256]{1,0:T(8,128)(2,1)S(1)}, bf16[256,256]{1,0:T(8,128)(2,1)}, u32[]{:S(2)}) copy-start(bf16[256,256]{1,0:T(8,128)(2,1)} %constant.6.clone.sy_ref) | copy-start | bytes 393220
  0.9 0.7 %copy-start.3 = (s32[1,4,16]{2,1,0:T(4,128)S(1)}, s32[1,4,16]{2,1,0:T(4,128)}, u32[]{:S(2)}) copy-start(s32[1,4,16]{2,1,0:T(4,128)} %param.11) | copy-start | bytes 772
  1.6 0.7 copy-start.6
  2.3 0.7 copy-start.7
  3.0 22.2 %copy-start.2 = (bf16[16,512]{1,0:T(8,128)(2,1)S(1)}, bf16[16,512]{1,0:T(8,128)(2,1)}, u32[]{:S(2)}) copy-start(bf16[16,512]{1,0:T(8,128)(2,1)} %constant.8.clone.sx_ref) | copy-start | bytes 49156
  3.0 30.2 %copy-start.1 = (bf16[384,128]{1,0:T(8,128)(2,1)S(1)}, bf16[384,128]{1,0:T(8,128)(2,1)}, u32[]{:S(2)}) copy-start(bf16[384,128]{1,0:T(8,128)(2,1)} %constant.7.clone.sz_ref) | copy-start | bytes 294916
  4.1 14.1 %all-to-all-start = ((s32[16,8,128]{2,1,0:T(8,128)}), s32[16,8,128]{2,1,0:T(8,128)S(1)}, u32[]{:S(2)}, u32[]{:S(2)}) async-start(s32[16,8,128]{2,1,0:T(8,128)} %get-tuple-element.17), calls=%async_computation | async-start | bytes 131072 | tf_op jit(solution)/shard_map/all_to_all | solution.py:395
  20.8 12.3 %all-to-all-start.1 = ((f32[16,40,128]{2,1,0:T(8,128)}), f32[16,40,128]{2,1,0:T(8,128)S(1)}, u32[]{:S(2)}, u32[]{:S(2)}) async-start(f32[16,40,128]{2,1,0:T(8,128)} %shard_map.84), calls=%async_computation.1 | async-start | bytes 655360 | tf_op jit(solution)/shard_map/all_to_all | solution.py:397

commit v3 on v2

--- a/solution.py
+++ b/solution.py
@@ -42,15 +42,13 @@
 
 
 def constants():
-    sy = signs(NY)
-    sy = np.concatenate([sy[0::2], sy[1::2]], axis=0)
     sz = np.zeros((LANES, LANES), np.float32)
     sz[:NZ, :NZ] = signs(NZ).T
     sz[NZ:, NZ:] = signs(NZ).T
     sz = np.concatenate([sz] * 3, axis=0)
     sx = np.repeat(signs(SLABS), COARSE, axis=1)
     bf = jnp.bfloat16
-    return np.asarray(sy, bf), np.asarray(sz, bf), np.asarray(sx, bf)
+    return np.asarray(sz, bf), np.asarray(sx, bf)
 
 
 def slab_pos():
@@ -110,10 +108,7 @@
     return lax.shift_right_logical(iota((ROWS, 1), 0), 4)
 
 
-def list_kernel(kept_ref, place_ref, height_ref, sy_ref, out_ref, place_out, height_out, sy_out):
-    sy_out[...] = sy_ref[...]
-    place_out[...] = place_ref[...]
-    height_out[...] = height_ref[...]
+def list_kernel(kept_ref, out_ref):
     k = column(kept_ref[...].astype(jnp.float32)).astype(jnp.int32)
     _, pair, xs, tab = places_of(k)
     table = station_col() * XL + tab
@@ -132,9 +127,25 @@
 PART = XL * NZ
 
 
-def table_kernel(place_ref, height_ref, w_hbm, sy_ref, far_ref, *refs):
+def haar_signs():
+    row = iota((NY, 1), 0)
+    b = 2 * (row & (NY // 2 - 1)) + lax.shift_right_logical(row, 7)
+    start = jnp.zeros_like(b)
+    width = jnp.full_like(b, NY)
+    for level in range(1, 8):
+        inside = b >= (1 << level)
+        width = jnp.where(inside, NY >> level, width)
+        start = jnp.where(inside, (b - (1 << level)) * (NY >> level), start)
+    middle = jnp.where(b == 0, start + width, start + lax.shift_right_logical(width, 1))
+    y = iota((NY, NY), 1)
+    signed = jnp.where(y < middle, 1.0, jnp.where(y < start + width, -1.0, 0.0))
+    signed = jnp.where(y < start, 0.0, signed).astype(jnp.bfloat16)
+    return jnp.concatenate([signed, signed], axis=1)
+
+
+def table_kernel(place_ref, height_ref, w_hbm, far_ref, *refs):
     outs = refs[: STA - 1]
-    w_ref, g_ref, own_ref, w_sems, sem = refs[STA - 1 :]
+    w_ref, sy_ref, g_ref, own_ref, w_sems, sem = refs[STA - 1 :]
     first = (slab_pos() * XL).astype(jnp.float32)
     yy = iota((1, NY), 1).astype(jnp.float32) + 0.5
     rows = 16
@@ -143,6 +154,7 @@
         at = (slice(None), pl.ds(i * rows, rows))
         arrivals.append(pltpu.make_async_copy(w_hbm.at[at], w_ref.at[at], w_sems.at[i]))
         arrivals[-1].start()
+    sy_ref[...] = haar_signs()
 
     def field(s):
         east0 = place_ref[0:1, s : s + 1] * float(NX)
@@ -182,7 +194,7 @@
         for i in range(PART // 256):
             g = g_ref[s * PART + i * 256 : s * PART + (i + 1) * 256, :]
             u = lax.dot_general(
-                jnp.concatenate([sy_ref[...]] * 2, axis=1),
+                sy_ref[...],
                 g,
                 (((1,), (1,)), ((), ())),
                 preferred_element_type=jnp.float32,
@@ -203,7 +215,8 @@
 
 
 def message_kernel(code_ref, far_ref, *refs):
-    u_refs, out_ref, near_ref, sem = refs[: STA - 1], refs[STA - 1], refs[STA], refs[STA + 1]
+    u_refs = refs[: STA - 1]
+    out_hbm, out_ref, near_ref, sems, sem = refs[STA - 1 :]
     copy = pltpu.make_async_copy(far_ref.at[0], near_ref, sem)
     copy.start()
     low_half = iota((16, 128), 1) < NZ
@@ -248,6 +261,7 @@
         for s in range(1, STA):
             coarse(g, s, u_refs[s - 1])
     copy.wait()
+    leaving = []
     for g in range(groups):
         coarse(g, 0, near_ref)
         both = got[g] + picked(g, (near_ref, u_refs[0]), 0)
@@ -256,6 +270,11 @@
         odd = jnp.where(low_half, pltpu.roll(v0, NZ, 1), v1)
         fine = jnp.where(known(g)[0] >= 512, odd, even)
         out_ref[2 * g : 2 * g + 2, COARSE:MSG, :] = fine.reshape(2, FINE, 128)
+        at = pl.ds(2 * g, 2)
+        leaving.append(pltpu.make_async_copy(out_ref.at[at], out_hbm.at[at], sems.at[g]))
+        leaving[-1].start()
+    for gone in leaving:
+        gone.wait()
 
 
 def power(level_top, value):
@@ -277,8 +296,8 @@
     key = jnp.where(xs < SLABS, xs * FINE + rank, -1)
     fine_ref[...] = jnp.where(iota((ROWS, SLABS * FINE), 1) == key, 1.0, 0.0).astype(jnp.bfloat16)
     dest = column(dest_ref[...].astype(jnp.float32))
-    spot = turned(dest * 8.0 + earlier(dest)).astype(jnp.int32)
-    where = jnp.broadcast_to(spot, (OWNERS * 8, ROWS)) == iota((OWNERS * 8, ROWS), 0)
+    spot = turned(earlier(dest) * float(OWNERS) + dest).astype(jnp.int32)
+    where = jnp.broadcast_to(spot, (OWNERS * CAP, ROWS)) == iota((OWNERS * CAP, ROWS), 0)
     spot_ref[...] = jnp.where(where, 1.0, 0.0).astype(jnp.bfloat16)
     b = 2 * (slab_pos() * HALF + pair)
     rowscale = power(8, a) * power(8, b)
@@ -300,11 +319,18 @@
     value = jnp.dot(jnp.concatenate(split(value, 3), axis=1), sz_ref[...], preferred_element_type=jnp.float32)
     value = value * scale_ref[...]
     placed = dots(spot_ref[...], split(value, 3))
-    out_ref[...] = placed.reshape(OWNERS, 8, LANES)
+    for slot in range(CAP):
+        rows = placed[slot * OWNERS : (slot + 1) * OWNERS]
+        out_ref[:, :, slot * LANES : (slot + 1) * LANES] = rows.reshape(OWNERS, 1, LANES)
 
 
 VMEM = pl.BlockSpec(memory_space=pltpu.VMEM)
 HBM = pl.BlockSpec(memory_space=pltpu.HBM)
+
+
+def finish_kernel(got_ref, out_ref):
+    for slot in range(CAP):
+        out_ref[slot] = got_ref[:, :, slot * LANES : (slot + 1) * LANES].reshape(OWNERS, LANES)
 
 
 def run(body, args, ins, shapes, outs, scratch=(), cost=None, limit=16 * MIB):
@@ -323,32 +349,23 @@
     return jax.ShapeDtypeStruct(shape, dtype)
 
 
-def lists(kept, place, height, sy):
-    return run(
-        list_kernel,
-        (kept, place.T, height.reshape(1, STA), sy),
-        [VMEM] * 4,
-        [
-            struct((SLABS, FINE, 128), jnp.int32),
-            struct((2, STA)),
-            struct((1, STA)),
-            struct((NY, NY), jnp.bfloat16),
-        ],
-        [VMEM] * 4,
-    )
-
-
-def tables(place, height, weight, sy):
+def lists(kept):
+    cost = pl.CostEstimate(flops=3 * 10**10, bytes_accessed=MIB, transcendentals=0)
+    return run(list_kernel, (kept,), [VMEM], struct((SLABS, FINE, 128), jnp.int32), VMEM, (), cost)
+
+
+def tables(place, height, weight):
     cost = pl.CostEstimate(flops=2 * 512 * 256 * 4096, bytes_accessed=6 * MIB, transcendentals=1 << 20)
     part = struct((NY, 2 * PART), jnp.bfloat16)
     return run(
         table_kernel,
-        (place, height, jnp.transpose(weight, (0, 2, 1)), sy),
-        [VMEM, VMEM, HBM, VMEM],
+        (place.T, height.reshape(1, STA), jnp.transpose(weight, (0, 2, 1))),
+        [VMEM, VMEM, HBM],
         [struct((FAR, NY, 2 * PART), jnp.bfloat16)] + [part] * (STA - 1),
         [HBM] + [VMEM] * (STA - 1),
         [
             pltpu.VMEM((XL, NZ, NY), jnp.float32),
+            pltpu.VMEM((NY, 2 * NY), jnp.bfloat16),
             pltpu.VMEM((TABS * NZ, 2 * NY), jnp.bfloat16),
             pltpu.VMEM((NY, 2 * PART), jnp.bfloat16),
             pltpu.SemaphoreType.DMA((NZ // 16,)),
@@ -365,8 +382,13 @@
         (codes, *u),
         [VMEM, HBM] + [VMEM] * (STA - 1),
         struct((SLABS, MSG, LANES)),
-        VMEM,
-        [pltpu.VMEM((NY, 2 * PART), jnp.bfloat16), pltpu.SemaphoreType.DMA],
+        HBM,
+        [
+            pltpu.VMEM((SLABS, MSG, LANES), jnp.float32),
+            pltpu.VMEM((NY, 2 * PART), jnp.bfloat16),
+            pltpu.SemaphoreType.DMA((SLABS // 2,)),
+            pltpu.SemaphoreType.DMA,
+        ],
         None,
         44 * MIB,
     )
@@ -377,27 +399,27 @@
     outs = [
         struct((ROWS, SLABS * COARSE), bf),
         struct((ROWS, SLABS * FINE), bf),
-        struct((OWNERS * 8, ROWS), bf),
+        struct((OWNERS * CAP, ROWS), bf),
         struct((ROWS, LANES)),
     ]
     return run(index_kernel, (kept, dest, sx), [VMEM] * 3, outs, [VMEM] * 4)
 
 
 def combined(got, index, sz):
-    return run(combine_kernel, (got, *index, sz), [VMEM] * 6, struct((OWNERS, 8, LANES)), VMEM)
+    return run(combine_kernel, (got, *index, sz), [VMEM] * 6, struct((OWNERS, 1, CAP * LANES)), VMEM)
 
 
 def local(station_place, station_height, cell_weight, kept, dest):
-    sy, sz, sx = (jnp.asarray(c) for c in constants())
+    sz, sx = (jnp.asarray(c) for c in constants())
     kept = kept.reshape(STA, KEEP)
     dest = dest.reshape(STA, KEEP)
-    codes, place, height, sy = lists(kept, station_place, station_height, sy)
-    codes = lax.all_to_all(codes, "slab", 0, 0, tiled=True)
-    u = tables(place, height, cell_weight, sy)
+    codes = lax.all_to_all(lists(kept), "slab", 0, 0, tiled=True)
+    u = tables(station_place, station_height, cell_weight)
     got = lax.all_to_all(messages(codes, u), "slab", 0, 0, tiled=True)
     index = indices(kept, dest, sx)
     out = lax.all_to_all(combined(got, index, sz), "sta", 0, 0, tiled=True)
-    return out[None, None, :, :CAP, :]
+    out = run(finish_kernel, (out,), [VMEM], struct((CAP, OWNERS, LANES)), VMEM)
+    return jnp.transpose(out, (1, 0, 2))[None, None]
 
 
 def solution(mesh):

time: 68.3 us -> 64.7 us (0.947)
  local copies, waits for them, and re-layouts: 3.63 us -> 0.7 us
  blocking collectives: 33.5 us -> 32.4 us
    unnamed x16 -> x14, local copies, waits for them, and re-layouts: 2.96 us -> 0.7 us
    all_to_all x1, blocking collectives: 33.5 us -> 32.4 us  [local(): out = lax.all_to_all(combined(got, index, sz), 'sta', 0, 0, tiled=True)]
    pallas_call x5 -> x6, Pallas kernels: 8.93 us -> 9.18 us  [run(): pl.pallas_call(body, out_shape=shapes, in_specs=ins, out_specs=outs, scra...]
where the time goes in v3:
time: 64.7 us; the launch traced here: 64.3 us
  blocking collectives  32.4 us (50%)
  starting transfers between devices  11.9 us (18%)
  waiting for transfers between devices  10 us (15%)
  Pallas kernels  9.18 us (14%)
  local copies, waits for them, and re-layouts  0.7 us (1%)
    all_to_all x1, blocking collectives, local(): out = lax.all_to_all(combined(got, index, sz), 'sta', 0, 0, tiled=True)  32.4 us
    pallas_call x6, Pallas kernels, run(): pl.pallas_call(body, out_shape=shapes, in_specs=ins, out_specs=outs, scra...  9.18 us
    all_to_all x1, starting transfers between devices, local(): codes = lax.all_to_all(lists(kept), 'slab', 0, 0, tiled=True)  7.73 us
    all_to_all x1, waiting for transfers between devices, local(): got = lax.all_to_all(messages(codes, u), 'slab', 0, 0, tiled=True)  7.47 us
    all_to_all x1, starting transfers between devices, local(): got = lax.all_to_all(messages(codes, u), 'slab', 0, 0, tiled=True)  4.14 us
    all_to_all x1, waiting for transfers between devices, local(): codes = lax.all_to_all(lists(kept), 'slab', 0, 0, tiled=True)  2.54 us
  transfers between devices with their start and end apart: 2, of which 2 were waited for; matrix products, arithmetic and copies ran while one was open for 0% of the time, Pallas kernels for 7%

profile of v3, /device:TPU:1, one launch (start us, length us, event | category | flops | bytes accessed | tf_op | source)
XLA Modules:
  0.0 64.3 jit_solution(6959625574653144585)
XLA Ops:
  0.0 0.0 copy-start.2
  0.0 0.7 %copy-done.2 = s32[1,4,16]{2,1,0:T(4,128)S(1)} copy-done((s32[1,4,16]{2,1,0:T(4,128)S(1)}, s32[1,4,16]{2,1,0:T(4,128)}, u32[]{:S(2)}) %copy-start.2) | copy-done | bytes 280
  0.7 0.0 copy-start.5
  0.7 0.0 copy-start.6
  0.7 1.1 %shard_map.73 = s32[16,8,128]{2,1,0:T(8,128)} custom-call(s32[4,16]{1,0:T(4,128)S(1)} %bitcast.8), custom_call_target="tpu_custom_call" | custom-call | flops 30000001024 | bytes 1048576 | tf_op jit(solution)/shard_map/pallas_call | solution.py:337
  1.8 0.0 copy-start.1
  1.8 0.0 copy-start.3
  1.8 0.0 copy-start.4
  1.8 0.0 copy-start
  1.8 7.7 %all-to-all-start = ((s32[16,8,128]{2,1,0:T(8,128)}), s32[16,8,128]{2,1,0:T(8,128)S(1)}, u32[]{:S(2)}, u32[]{:S(2)}) async-start(s32[16,8,128]{2,1,0:T(8,128)} %shard_map.73), calls=%async_computation | async-start | bytes 131072 | tf_op jit(solution)/shard_map/all_to_all | solution.py:416
  9.5 0.0 copy-done.5
  9.5 0.0 copy-done.6
  9.6 3.9 %shard_map.74 = (bf16[30,256,2048]{2,1,0:T(8,128)(2,1)}, bf16[256,2048]{1,0:T(8,128)(2,1)S(1)}, bf16[256,2048]{1,0:T(8,128)(2,1)S(1)}, bf16[256,2048]{1,0:T(8,128)(2,1)S(1)}) custom-call(f32[2,4]{1,0:T(2,128)S(1)} %bitcast.11, f32[1,4]{1,0:T(1,128)S(1)} %bitcast.12, f32[16,64,256]{2,1,0:T(8,128)} %bitcast.13), custom_call_target="tpu_custom_call" | custom-call | flops 1073741824 | bytes 6291456 | tf_op jit(solution)/shard_map/pallas_call | solution.py:337
  13.5 2.5 %all-to-all-done.code_ref = s32[16,8,128]{2,1,0:T(8,128)S(1)} async-done(((s32[16,8,128]{2,1,0:T(8,128)}), s32[16,8,128]{2,1,0:T(8,128)S(1)}, u32[]{:S(2)}, u32[]{:S(2)}) %all-to-all-start) | async-done | bytes 65568 | tf_op jit(solution)/shard_map/all_to_all | solution.py:416
  16.1 2.4 %shard_map.75 = f32[16,40,128]{2,1,0:T(8,128)} custom-call(s32[16,8,128]{2,1,0:T(8,128)S(1)} %all-to-all-done.code_ref, bf16[30,256,2048]{2,1,0:T(8,128)(2,1)} %get-tuple-element.13.far_ref, bf16[256,2048]{1,0:T(8,128)(2,1)S(1)} %get-tuple-element.14.refs_0_, bf16[256,2048]{1,0:T(8,128)(2,1)S(1)} %get-tuple-element.15.refs_1_, ...), custom_call_target="tpu_custom_call" | custom-call | tf_op jit(solution)/shard_map/pallas_call | solution.py:337
  18.5 4.1 %all-to-all-start.1 = ((f32[16,40,128]{2,1,0:T(8,128)}), f32[16,40,128]{2,1,0:T(8,128)S(1)}, u32[]{:S(2)}, u32[]{:S(2)}) async-start(f32[16,40,128]{2,1,0:T(8,128)} %shard_map.75), calls=%async_computation.1 | async-start | bytes 655360 | tf_op jit(solution)/shard_map/all_to_all | solution.py:418
  22.6 0.0 copy-done.1
  22.6 0.0 copy-done.3
  22.7 0.0 copy-done.4
  22.7 0.4 shard_map.76
  23.1 7.5 %all-to-all-done.1.got_ref = f32[16,40,128]{2,1,0:T(8,128)S(1)} async-done(((f32[16,40,128]{2,1,0:T(8,128)}), f32[16,40,128]{2,1,0:T(8,128)S(1)}, u32[]{:S(2)}, u32[]{:S(2)}) %all-to-all-start.1) | async-done | bytes 327712 | tf_op jit(solution)/shard_map/all_to_all | solution.py:418
  30.6 0.0 copy-done
  30.6 0.6 shard_map.77
  31.2 32.4 %all_to_all.15.got_ref = f32[32,1,768]{2,1,0:T(1,128)S(1)} all-to-all(f32[32,1,768]{2,1,0:T(1,128)S(1)} %shard_map.77), channel_id=1, replica_groups=mesh['slab'=16,'sta'=32] {'sta'}, dimensions={0} | all-to-all | bytes 196608 | tf_op jit(solution)/shard_map/all_to_all | solution.py:420
  63.6 0.7 %shard_map.78 = f32[6,32,128]{2,1,0:T(8,128)} custom-call(f32[32,1,768]{2,1,0:T(1,128)S(1)} %all_to_all.15.got_ref), custom_call_target="tpu_custom_call" | custom-call | tf_op jit(solution)/shard_map/pallas_call | solution.py:337
Async XLA Ops:
  0.0 0.7 %copy-start.2 = (s32[1,4,16]{2,1,0:T(4,128)S(1)}, s32[1,4,16]{2,1,0:T(4,128)}, u32[]{:S(2)}) copy-start(s32[1,4,16]{2,1,0:T(4,128)} %param.10) | copy-start | bytes 772
  0.7 8.9 %copy-start.5 = (f32[4,2]{0,1:T(2,128)S(1)}, f32[4,2]{0,1:T(2,128)}, u32[]{:S(2)}) copy-start(f32[4,2]{0,1:T(2,128)} %param.7) | copy-start | bytes 100
  0.7 8.9 %copy-start.6 = (f32[4]{0:T(128)S(1)}, f32[4]{0:T(128)}, u32[]{:S(2)}) copy-start(f32[4]{0:T(128)} %param.8) | copy-start | bytes 52
  1.8 20.8 %copy-start.1 = (bf16[16,512]{1,0:T(8,128)(2,1)S(1)}, bf16[16,512]{1,0:T(8,128)(2,1)}, u32[]{:S(2)}) copy-start(bf16[16,512]{1,0:T(8,128)(2,1)} %constant.5.clone.sx_ref) | copy-start | bytes 49156
  1.8 20.9 %copy-start.3 = (s32[1,4,16]{2,1,0:T(4,128)S(1)}, s32[1,4,16]{2,1,0:T(4,128)}, u32[]{:S(2)}) copy-start(s32[1,4,16]{2,1,0:T(4,128)} %param.10) | copy-start | bytes 772
  1.8 20.9 %copy-start.4 = (s32[1,4,16,1]{2,3,1,0:T(1,128)S(1)}, s32[1,4,16,1]{2,3,1,0:T(1,128)}, u32[]{:S(2)}) copy-start(s32[1,4,16,1]{2,3,1,0:T(1,128)} %param.11) | copy-start | bytes 772
  1.8 28.8 %copy-start = (bf16[384,128]{1,0:T(8,128)(2,1)S(1)}, bf16[384,128]{1,0:T(8,128)(2,1)}, u32[]{:S(2)}) copy-start(bf16[384,128]{1,0:T(8,128)(2,1)} %constant.4.clone.sz_ref) | copy-start | bytes 294916
  1.8 14.3 %all-to-all-start = ((s32[16,8,128]{2,1,0:T(8,128)}), s32[16,8,128]{2,1,0:T(8,128)S(1)}, u32[]{:S(2)}, u32[]{:S(2)}) async-start(s32[16,8,128]{2,1,0:T(8,128)} %shard_map.73), calls=%async_computation | async-start | bytes 131072 | tf_op jit(solution)/shard_map/all_to_all | solution.py:416
  18.5 12.1 %all-to-all-start.1 = ((f32[16,40,128]{2,1,0:T(8,128)}), f32[16,40,128]{2,1,0:T(8,128)S(1)}, u32[]{:S(2)}, u32[]{:S(2)}) async-start(f32[16,40,128]{2,1,0:T(8,128)} %shard_map.75), calls=%async_computation.1 | async-start | bytes 655360 | tf_op jit(solution)/shard_map/all_to_all | solution.py:418

commit v4 on v3

--- a/solution.py
+++ b/solution.py
@@ -145,7 +145,7 @@
 
 def table_kernel(place_ref, height_ref, w_hbm, far_ref, *refs):
     outs = refs[: STA - 1]
-    w_ref, sy_ref, g_ref, own_ref, w_sems, sem = refs[STA - 1 :]
+    w_ref, ready_ref, sy_ref, g_ref, own_ref, w_sems, sem = refs[STA - 1 :]
     first = (slab_pos() * XL).astype(jnp.float32)
     yy = iota((1, NY), 1).astype(jnp.float32) + 0.5
     rows = 16
@@ -160,17 +160,24 @@
         east0 = place_ref[0:1, s : s + 1] * float(NX)
         north2 = (yy - place_ref[1:2, s : s + 1] * float(NY)) ** 2
         height = height_ref[0:1, s : s + 1]
+
+        def cells(x, z0):
+            zz = (z0 + iota((rows, 1), 0)).astype(jnp.float32) + 0.5 + height
+            east = (first + (x + 0.5)) - east0
+            r = lax.rsqrt((north2 + zz * zz) + east * east)
+            return jnp.broadcast_to(SCALE * zz, (rows, NY)) * (r * r * r)
+
+        if s == 0:
+            for z0 in range(0, NZ, rows):
+                for x in range(XL):
+                    ready_ref[x, z0 : z0 + rows, :] = cells(x, z0)
         for z0 in range(0, NZ, rows):
             if s == 0:
                 arrivals[z0 // rows].wait()
-            zz = (z0 + iota((rows, 1), 0)).astype(jnp.float32) + 0.5 + height
-            base = north2 + zz * zz
-            lead = jnp.broadcast_to(SCALE * zz, (rows, NY))
 
             def leaf(x):
-                east = (first + (x + 0.5)) - east0
-                r = lax.rsqrt(base + east * east)
-                return (w_ref[x, z0 : z0 + rows, :] * lead) * (r * r * r)
+                known = ready_ref[x, z0 : z0 + rows, :] if s == 0 else cells(x, z0)
+                return w_ref[x, z0 : z0 + rows, :] * known
 
             def put(tab, value):
                 at = slice((s * XL + tab) * NZ + z0, (s * XL + tab) * NZ + z0 + rows)
@@ -216,9 +223,10 @@
 
 def message_kernel(code_ref, far_ref, *refs):
     u_refs = refs[: STA - 1]
-    out_hbm, out_ref, near_ref, sems, sem = refs[STA - 1 :]
+    kept_ref, dest_ref, sx_ref, out_ref, coarse_ref, fine_ref, spot_ref, scale_ref, near_ref, sem = refs[STA - 1 :]
     copy = pltpu.make_async_copy(far_ref.at[0], near_ref, sem)
     copy.start()
+    index_kernel(kept_ref, dest_ref, sx_ref, coarse_ref, fine_ref, spot_ref, scale_ref)
     low_half = iota((16, 128), 1) < NZ
     column_id = iota((16, 256), 1)
     groups = SLABS // 2
@@ -261,7 +269,6 @@
         for s in range(1, STA):
             coarse(g, s, u_refs[s - 1])
     copy.wait()
-    leaving = []
     for g in range(groups):
         coarse(g, 0, near_ref)
         both = got[g] + picked(g, (near_ref, u_refs[0]), 0)
@@ -270,11 +277,6 @@
         odd = jnp.where(low_half, pltpu.roll(v0, NZ, 1), v1)
         fine = jnp.where(known(g)[0] >= 512, odd, even)
         out_ref[2 * g : 2 * g + 2, COARSE:MSG, :] = fine.reshape(2, FINE, 128)
-        at = pl.ds(2 * g, 2)
-        leaving.append(pltpu.make_async_copy(out_ref.at[at], out_hbm.at[at], sems.at[g]))
-        leaving[-1].start()
-    for gone in leaving:
-        gone.wait()
 
 
 def power(level_top, value):
@@ -365,6 +367,7 @@
         [HBM] + [VMEM] * (STA - 1),
         [
             pltpu.VMEM((XL, NZ, NY), jnp.float32),
+            pltpu.VMEM((XL, NZ, NY), jnp.float32),
             pltpu.VMEM((NY, 2 * NY), jnp.bfloat16),
             pltpu.VMEM((TABS * NZ, 2 * NY), jnp.bfloat16),
             pltpu.VMEM((NY, 2 * PART), jnp.bfloat16),
@@ -376,33 +379,25 @@
     )
 
 
-def messages(codes, u):
-    return run(
-        message_kernel,
-        (codes, *u),
-        [VMEM, HBM] + [VMEM] * (STA - 1),
-        struct((SLABS, MSG, LANES)),
-        HBM,
-        [
-            pltpu.VMEM((SLABS, MSG, LANES), jnp.float32),
-            pltpu.VMEM((NY, 2 * PART), jnp.bfloat16),
-            pltpu.SemaphoreType.DMA((SLABS // 2,)),
-            pltpu.SemaphoreType.DMA,
-        ],
-        None,
-        44 * MIB,
-    )
-
-
-def indices(kept, dest, sx):
+def messages(codes, u, kept, dest, sx):
     bf = jnp.bfloat16
     outs = [
+        struct((SLABS, MSG, LANES)),
         struct((ROWS, SLABS * COARSE), bf),
         struct((ROWS, SLABS * FINE), bf),
         struct((OWNERS * CAP, ROWS), bf),
         struct((ROWS, LANES)),
     ]
-    return run(index_kernel, (kept, dest, sx), [VMEM] * 3, outs, [VMEM] * 4)
+    return run(
+        message_kernel,
+        (codes, *u, kept, dest, sx),
+        [VMEM, HBM] + [VMEM] * (STA + 2),
+        outs,
+        [VMEM] * 5,
+        [pltpu.VMEM((NY, 2 * PART), bf), pltpu.SemaphoreType.DMA],
+        None,
+        44 * MIB,
+    )
 
 
 def combined(got, index, sz):
@@ -415,8 +410,8 @@
     dest = dest.reshape(STA, KEEP)
     codes = lax.all_to_all(lists(kept), "slab", 0, 0, tiled=True)
     u = tables(station_place, station_height, cell_weight)
-    got = lax.all_to_all(messages(codes, u), "slab", 0, 0, tiled=True)
-    index = indices(kept, dest, sx)
+    rows, *index = messages(codes, u, kept, dest, sx)
+    got = lax.all_to_all(rows, "slab", 0, 0, tiled=True)
     out = lax.all_to_all(combined(got, index, sz), "sta", 0, 0, tiled=True)
     out = run(finish_kernel, (out,), [VMEM], struct((CAP, OWNERS, LANES)), VMEM)
     return jnp.transpose(out, (1, 0, 2))[None, None]

time: 64.7 us -> 63.6 us (0.983)
  blocking collectives: 32.4 us -> 44.2 us
  waiting for transfers between devices: 10 us -> 2.63 us
  starting transfers between devices: 11.9 us -> 7.72 us
  Pallas kernels: 9.18 us -> 7.98 us
    all_to_all x0 -> x1, blocking collectives: none -> 11.8 us  [local(): got = lax.all_to_all(rows, 'slab', 0, 0, tiled=True)]
    all_to_all x1 -> x0, waiting for transfers between devices: 7.47 us -> none  [local(): got = lax.all_to_all(messages(codes, u), 'slab', 0, 0, tiled=True)]
    all_to_all x1 -> x0, starting transfers between devices: 4.14 us -> none  [local(): got = lax.all_to_all(messages(codes, u), 'slab', 0, 0, tiled=True)]
    pallas_call x6 -> x5, Pallas kernels: 9.18 us -> 7.98 us  [run(): pl.pallas_call(body, out_shape=shapes, in_specs=ins, out_specs=outs, scra...]
  transfers between devices with their start and end apart: 2 -> 1, of which waited for: 2 -> 1; matrix products, arithmetic and copies ran while one was open for 0% -> 0% of each run, Pallas kernels for 7% -> 6%
where the time goes in v4:
time: 63.6 us; the launch traced here: 63.3 us
  blocking collectives  44.2 us (69%)
  Pallas kernels  7.98 us (13%)
  starting transfers between devices  7.72 us (12%)
  waiting for transfers between devices  2.63 us (4%)
  local copies, waits for them, and re-layouts  0.7 us (1%)
    all_to_all x1, blocking collectives, local(): out = lax.all_to_all(combined(got, index, sz), 'sta', 0, 0, tiled=True)  32.4 us
    all_to_all x1, blocking collectives, local(): got = lax.all_to_all(rows, 'slab', 0, 0, tiled=True)  11.8 us
    pallas_call x5, Pallas kernels, run(): pl.pallas_call(body, out_shape=shapes, in_specs=ins, out_specs=outs, scra...  7.98 us
    all_to_all x1, starting transfers between devices, local(): codes = lax.all_to_all(lists(kept), 'slab', 0, 0, tiled=True)  7.72 us
    all_to_all x1, waiting for transfers between devices, local(): codes = lax.all_to_all(lists(kept), 'slab', 0, 0, tiled=True)  2.63 us
  transfers between devices with their start and end apart: 1, of which 1 were waited for; matrix products, arithmetic and copies ran while one was open for 0% of the time, Pallas kernels for 6%

profile of v4, /device:TPU:1, one launch (start us, length us, event | category | flops | bytes accessed | tf_op | source)
XLA Modules:
  0.0 63.3 jit_solution(8643608540376120913)
XLA Ops:
  0.0 0.0 copy-start.2
  0.0 0.7 %copy-done.2 = s32[1,4,16]{2,1,0:T(4,128)S(1)} copy-done((s32[1,4,16]{2,1,0:T(4,128)S(1)}, s32[1,4,16]{2,1,0:T(4,128)}, u32[]{:S(2)}) %copy-start.2) | copy-done | bytes 280
  0.7 0.0 copy-start.5
  0.7 0.0 copy-start.6
  0.7 0.0 copy-start.1
  0.7 0.0 copy-start.3
  0.7 0.0 copy-start.4
  0.7 1.1 %shard_map.73 = s32[16,8,128]{2,1,0:T(8,128)} custom-call(s32[4,16]{1,0:T(4,128)S(1)} %bitcast.8), custom_call_target="tpu_custom_call" | custom-call | flops 30000001024 | bytes 1048576 | tf_op jit(solution)/shard_map/pallas_call | solution.py:339
  1.8 0.0 copy-start
  1.8 7.7 %all-to-all-start = ((s32[16,8,128]{2,1,0:T(8,128)}), s32[16,8,128]{2,1,0:T(8,128)S(1)}, u32[]{:S(2)}, u32[]{:S(2)}) async-start(s32[16,8,128]{2,1,0:T(8,128)} %shard_map.73), calls=%async_computation | async-start | bytes 131072 | tf_op jit(solution)/shard_map/all_to_all | solution.py:411
  9.5 0.0 copy-done.5
  9.5 0.0 copy-done.6
  9.6 3.9 %shard_map.74 = (bf16[30,256,2048]{2,1,0:T(8,128)(2,1)}, bf16[256,2048]{1,0:T(8,128)(2,1)S(1)}, bf16[256,2048]{1,0:T(8,128)(2,1)S(1)}, bf16[256,2048]{1,0:T(8,128)(2,1)S(1)}) custom-call(f32[2,4]{1,0:T(2,128)S(1)} %bitcast.11, f32[1,4]{1,0:T(1,128)S(1)} %bitcast.12, f32[16,64,256]{2,1,0:T(8,128)} %bitcast.13), custom_call_target="tpu_custom_call" | custom-call | flops 1073741824 | bytes 6291456 | tf_op jit(solution)/shard_map/pallas_call | solution.py:339
  13.4 2.6 %all-to-all-done.code_ref = s32[16,8,128]{2,1,0:T(8,128)S(1)} async-done(((s32[16,8,128]{2,1,0:T(8,128)}), s32[16,8,128]{2,1,0:T(8,128)S(1)}, u32[]{:S(2)}, u32[]{:S(2)}) %all-to-all-start) | async-done | bytes 65568 | tf_op jit(solution)/shard_map/all_to_all | solution.py:411
  16.0 0.0 copy-done.1
  16.1 0.0 copy-done.3
  16.1 0.0 copy-done.4
  16.1 1.7 %shard_map.75 = (f32[16,40,128]{2,1,0:T(8,128)S(1)}, bf16[64,512]{1,0:T(8,128)(2,1)S(1)}, bf16[64,128]{1,0:T(8,128)(2,1)S(1)}, bf16[192,64]{1,0:T(8,128)(2,1)S(1)}, f32[64,128]{1,0:T(8,128)S(1)}) custom-call(s32[16,8,128]{2,1,0:T(8,128)S(1)} %all-to-all-done.code_ref, bf16[30,256,2048]{2,1,0:T(8,128)(2,1)} %get-tuple-element.14.far_ref, ...), custom_call_target="tpu_custom_call" | custom-call | tf_op jit(solution)/shard_map/pallas_call | solution.py:339
  17.8 11.8 %all_to_all.15.got_ref = f32[16,40,128]{2,1,0:T(8,128)S(1)} all-to-all(f32[16,40,128]{2,1,0:T(8,128)S(1)} %get-tuple-element.18), channel_id=1, replica_groups=mesh['slab'=16,'sta'=32] {'slab'}, dimensions={0} | all-to-all | bytes 655360 | tf_op jit(solution)/shard_map/all_to_all | solution.py:414
  29.6 0.0 copy-done
  29.6 0.6 shard_map.76
  30.2 32.4 %all_to_all.16.got_ref = f32[32,1,768]{2,1,0:T(1,128)S(1)} all-to-all(f32[32,1,768]{2,1,0:T(1,128)S(1)} %shard_map.76), channel_id=1, replica_groups=mesh['slab'=16,'sta'=32] {'sta'}, dimensions={0} | all-to-all | bytes 196608 | tf_op jit(solution)/shard_map/all_to_all | solution.py:415
  62.6 0.7 %shard_map.77 = f32[6,32,128]{2,1,0:T(8,128)} custom-call(f32[32,1,768]{2,1,0:T(1,128)S(1)} %all_to_all.16.got_ref), custom_call_target="tpu_custom_call" | custom-call | tf_op jit(solution)/shard_map/pallas_call | solution.py:339
Async XLA Ops:
  0.0 0.7 %copy-start.2 = (s32[1,4,16]{2,1,0:T(4,128)S(1)}, s32[1,4,16]{2,1,0:T(4,128)}, u32[]{:S(2)}) copy-start(s32[1,4,16]{2,1,0:T(4,128)} %param.10) | copy-start | bytes 772
  0.7 8.8 %copy-start.5 = (f32[4,2]{0,1:T(2,128)S(1)}, f32[4,2]{0,1:T(2,128)}, u32[]{:S(2)}) copy-start(f32[4,2]{0,1:T(2,128)} %param.7) | copy-start | bytes 100
  0.7 8.9 %copy-start.6 = (f32[4]{0:T(128)S(1)}, f32[4]{0:T(128)}, u32[]{:S(2)}) copy-start(f32[4]{0:T(128)} %param.8) | copy-start | bytes 52
  0.7 15.4 %copy-start.1 = (bf16[16,512]{1,0:T(8,128)(2,1)S(1)}, bf16[16,512]{1,0:T(8,128)(2,1)}, u32[]{:S(2)}) copy-start(bf16[16,512]{1,0:T(8,128)(2,1)} %constant.5.clone.refs_5_) | copy-start | bytes 49156
  0.7 15.4 %copy-start.3 = (s32[1,4,16]{2,1,0:T(4,128)S(1)}, s32[1,4,16]{2,1,0:T(4,128)}, u32[]{:S(2)}) copy-start(s32[1,4,16]{2,1,0:T(4,128)} %param.10) | copy-start | bytes 772
  0.7 15.4 %copy-start.4 = (s32[1,4,16,1]{2,3,1,0:T(1,128)S(1)}, s32[1,4,16,1]{2,3,1,0:T(1,128)}, u32[]{:S(2)}) copy-start(s32[1,4,16,1]{2,3,1,0:T(1,128)} %param.11) | copy-start | bytes 772
  1.8 27.8 %copy-start = (bf16[384,128]{1,0:T(8,128)(2,1)S(1)}, bf16[384,128]{1,0:T(8,128)(2,1)}, u32[]{:S(2)}) copy-start(bf16[384,128]{1,0:T(8,128)(2,1)} %constant.4.clone.sz_ref) | copy-start | bytes 294916
  1.8 14.2 %all-to-all-start = ((s32[16,8,128]{2,1,0:T(8,128)}), s32[16,8,128]{2,1,0:T(8,128)S(1)}, u32[]{:S(2)}, u32[]{:S(2)}) async-start(s32[16,8,128]{2,1,0:T(8,128)} %shard_map.73), calls=%async_computation | async-start | bytes 131072 | tf_op jit(solution)/shard_map/all_to_all | solution.py:411

commit v5 on v4

--- a/solution.py
+++ b/solution.py
@@ -228,7 +228,6 @@
     copy.start()
     index_kernel(kept_ref, dest_ref, sx_ref, coarse_ref, fine_ref, spot_ref, scale_ref)
     low_half = iota((16, 128), 1) < NZ
-    column_id = iota((16, 256), 1)
     groups = SLABS // 2
 
     def rows_of(g, t):
@@ -236,11 +235,11 @@
 
     def known(g):
         code = code_ref[2 * g : 2 * g + 2].reshape(16, 128)
-        wide = jnp.concatenate([code, code], axis=1)
-        return code, jnp.where(wide >= 0, wide & 511, -1)
+        return code, jnp.where(code >= 0, code & 511, -1)
 
     def picked(g, tables, base):
-        pick = jnp.where(known(g)[1] == column_id + base, 1.0, 0.0).astype(jnp.bfloat16)
+        wide = jnp.concatenate([known(g)[1]] * len(tables), axis=1)
+        pick = jnp.where(wide == iota(wide.shape, 1) + base, 1.0, 0.0).astype(jnp.bfloat16)
         total = None
         for part in (0, PART):
             both = []
@@ -264,14 +263,14 @@
         row = jnp.where(low_half, pltpu.roll(v[0], NZ, 1), v[1])
         out_ref[2 * g : 2 * g + 2, s * HALF : (s + 1) * HALF, :] = row.reshape(2, HALF, 128)
 
-    got = [picked(g, u_refs[1:], 256) for g in range(groups)]
+    got = [picked(g, u_refs[1:], 256) + picked(g, u_refs[:1], 128) for g in range(groups)]
     for g in range(groups):
         for s in range(1, STA):
             coarse(g, s, u_refs[s - 1])
     copy.wait()
     for g in range(groups):
         coarse(g, 0, near_ref)
-        both = got[g] + picked(g, (near_ref, u_refs[0]), 0)
+        both = got[g] + picked(g, (near_ref,), 0)
         v0, v1 = both[:, :128], both[:, 128:]
         even = jnp.where(low_half, v0, pltpu.roll(v1, NZ, 1))
         odd = jnp.where(low_half, pltpu.roll(v0, NZ, 1), v1)

time: 63.6 us -> 63.8 us (level)
  no operation moved by 1% of the time
where the time goes in v5:
time: 63.8 us; the launch traced here: 63.5 us
  blocking collectives  44.2 us (69%)
  Pallas kernels  8.17 us (13%)
  starting transfers between devices  7.72 us (12%)
  waiting for transfers between devices  2.63 us (4%)
  local copies, waits for them, and re-layouts  0.7 us (1%)
    all_to_all x1, blocking collectives, local(): out = lax.all_to_all(combined(got, index, sz), 'sta', 0, 0, tiled=True)  32.4 us
    all_to_all x1, blocking collectives, local(): got = lax.all_to_all(rows, 'slab', 0, 0, tiled=True)  11.8 us
    pallas_call x5, Pallas kernels, run(): pl.pallas_call(body, out_shape=shapes, in_specs=ins, out_specs=outs, scra...  8.17 us
    all_to_all x1, starting transfers between devices, local(): codes = lax.all_to_all(lists(kept), 'slab', 0, 0, tiled=True)  7.72 us
    all_to_all x1, waiting for transfers between devices, local(): codes = lax.all_to_all(lists(kept), 'slab', 0, 0, tiled=True)  2.63 us
  transfers between devices with their start and end apart: 1, of which 1 were waited for; matrix products, arithmetic and copies ran while one was open for 0% of the time, Pallas kernels for 6%

profile of v5, /device:TPU:1, one launch (start us, length us, event | category | flops | bytes accessed | tf_op | source)
XLA Modules:
  0.0 63.5 jit_solution(15484324659102666409)
XLA Ops:
  0.0 0.0 copy-start.2
  0.0 0.7 %copy-done.2 = s32[1,4,16]{2,1,0:T(4,128)S(1)} copy-done((s32[1,4,16]{2,1,0:T(4,128)S(1)}, s32[1,4,16]{2,1,0:T(4,128)}, u32[]{:S(2)}) %copy-start.2) | copy-done | bytes 280
  0.7 0.0 copy-start.5
  0.7 0.0 copy-start.6
  0.7 0.0 copy-start.1
  0.7 0.0 copy-start.3
  0.7 0.0 copy-start.4
  0.7 1.1 %shard_map.73 = s32[16,8,128]{2,1,0:T(8,128)} custom-call(s32[4,16]{1,0:T(4,128)S(1)} %bitcast.8), custom_call_target="tpu_custom_call" | custom-call | flops 30000001024 | bytes 1048576 | tf_op jit(solution)/shard_map/pallas_call | solution.py:338
  1.8 0.0 copy-start
  1.8 7.7 %all-to-all-start = ((s32[16,8,128]{2,1,0:T(8,128)}), s32[16,8,128]{2,1,0:T(8,128)S(1)}, u32[]{:S(2)}, u32[]{:S(2)}) async-start(s32[16,8,128]{2,1,0:T(8,128)} %shard_map.73), calls=%async_computation | async-start | bytes 131072 | tf_op jit(solution)/shard_map/all_to_all | solution.py:410
  9.5 0.0 copy-done.5
  9.5 0.0 copy-done.6
  9.6 3.9 %shard_map.74 = (bf16[30,256,2048]{2,1,0:T(8,128)(2,1)}, bf16[256,2048]{1,0:T(8,128)(2,1)S(1)}, bf16[256,2048]{1,0:T(8,128)(2,1)S(1)}, bf16[256,2048]{1,0:T(8,128)(2,1)S(1)}) custom-call(f32[2,4]{1,0:T(2,128)S(1)} %bitcast.11, f32[1,4]{1,0:T(1,128)S(1)} %bitcast.12, f32[16,64,256]{2,1,0:T(8,128)} %bitcast.13), custom_call_target="tpu_custom_call" | custom-call | flops 1073741824 | bytes 6291456 | tf_op jit(solution)/shard_map/pallas_call | solution.py:338
  13.4 2.6 %all-to-all-done.code_ref = s32[16,8,128]{2,1,0:T(8,128)S(1)} async-done(((s32[16,8,128]{2,1,0:T(8,128)}), s32[16,8,128]{2,1,0:T(8,128)S(1)}, u32[]{:S(2)}, u32[]{:S(2)}) %all-to-all-start) | async-done | bytes 65568 | tf_op jit(solution)/shard_map/all_to_all | solution.py:410
  16.0 0.0 copy-done.1
  16.1 0.0 copy-done.3
  16.1 0.0 copy-done.4
  16.1 1.9 %shard_map.75 = (f32[16,40,128]{2,1,0:T(8,128)S(1)}, bf16[64,512]{1,0:T(8,128)(2,1)S(1)}, bf16[64,128]{1,0:T(8,128)(2,1)S(1)}, bf16[192,64]{1,0:T(8,128)(2,1)S(1)}, f32[64,128]{1,0:T(8,128)S(1)}) custom-call(s32[16,8,128]{2,1,0:T(8,128)S(1)} %all-to-all-done.code_ref, bf16[30,256,2048]{2,1,0:T(8,128)(2,1)} %get-tuple-element.14.far_ref, ...), custom_call_target="tpu_custom_call" | custom-call | tf_op jit(solution)/shard_map/pallas_call | solution.py:338
  18.0 11.8 %all_to_all.15.got_ref = f32[16,40,128]{2,1,0:T(8,128)S(1)} all-to-all(f32[16,40,128]{2,1,0:T(8,128)S(1)} %get-tuple-element.18), channel_id=1, replica_groups=mesh['slab'=16,'sta'=32] {'slab'}, dimensions={0} | all-to-all | bytes 655360 | tf_op jit(solution)/shard_map/all_to_all | solution.py:413
  29.8 0.0 copy-done
  29.8 0.6 shard_map.76
  30.4 32.4 %all_to_all.16.got_ref = f32[32,1,768]{2,1,0:T(1,128)S(1)} all-to-all(f32[32,1,768]{2,1,0:T(1,128)S(1)} %shard_map.76), channel_id=1, replica_groups=mesh['slab'=16,'sta'=32] {'sta'}, dimensions={0} | all-to-all | bytes 196608 | tf_op jit(solution)/shard_map/all_to_all | solution.py:414
  62.8 0.7 %shard_map.77 = f32[6,32,128]{2,1,0:T(8,128)} custom-call(f32[32,1,768]{2,1,0:T(1,128)S(1)} %all_to_all.16.got_ref), custom_call_target="tpu_custom_call" | custom-call | tf_op jit(solution)/shard_map/pallas_call | solution.py:338
Async XLA Ops:
  0.0 0.7 %copy-start.2 = (s32[1,4,16]{2,1,0:T(4,128)S(1)}, s32[1,4,16]{2,1,0:T(4,128)}, u32[]{:S(2)}) copy-start(s32[1,4,16]{2,1,0:T(4,128)} %param.10) | copy-start | bytes 772
  0.7 8.8 %copy-start.5 = (f32[4,2]{0,1:T(2,128)S(1)}, f32[4,2]{0,1:T(2,128)}, u32[]{:S(2)}) copy-start(f32[4,2]{0,1:T(2,128)} %param.7) | copy-start | bytes 100
  0.7 8.9 %copy-start.6 = (f32[4]{0:T(128)S(1)}, f32[4]{0:T(128)}, u32[]{:S(2)}) copy-start(f32[4]{0:T(128)} %param.8) | copy-start | bytes 52
  0.7 15.4 %copy-start.1 = (bf16[16,512]{1,0:T(8,128)(2,1)S(1)}, bf16[16,512]{1,0:T(8,128)(2,1)}, u32[]{:S(2)}) copy-start(bf16[16,512]{1,0:T(8,128)(2,1)} %constant.5.clone.refs_5_) | copy-start | bytes 49156
  0.7 15.4 %copy-start.3 = (s32[1,4,16]{2,1,0:T(4,128)S(1)}, s32[1,4,16]{2,1,0:T(4,128)}, u32[]{:S(2)}) copy-start(s32[1,4,16]{2,1,0:T(4,128)} %param.10) | copy-start | bytes 772
  0.7 15.4 %copy-start.4 = (s32[1,4,16,1]{2,3,1,0:T(1,128)S(1)}, s32[1,4,16,1]{2,3,1,0:T(1,128)}, u32[]{:S(2)}) copy-start(s32[1,4,16,1]{2,3,1,0:T(1,128)} %param.11) | copy-start | bytes 772
  1.8 28.0 %copy-start = (bf16[384,128]{1,0:T(8,128)(2,1)S(1)}, bf16[384,128]{1,0:T(8,128)(2,1)}, u32[]{:S(2)}) copy-start(bf16[384,128]{1,0:T(8,128)(2,1)} %constant.4.clone.sz_ref) | copy-start | bytes 294916
  1.8 14.2 %all-to-all-start = ((s32[16,8,128]{2,1,0:T(8,128)}), s32[16,8,128]{2,1,0:T(8,128)S(1)}, u32[]{:S(2)}, u32[]{:S(2)}) async-start(s32[16,8,128]{2,1,0:T(8,128)} %shard_map.73), calls=%async_computation | async-start | bytes 131072 | tf_op jit(solution)/shard_map/all_to_all | solution.py:410
